TPU v7x, 32 devices: a whole 2x2x4 slice. The times are simulated.
32 devices in a mesh: dp: 2 (over x), ctx: 8 (over z, y), head: 2 (over core).
Axes of the slice: x: 2, y: 2, z: 4, core: 2. Of those that a mesh axis runs over, the one named last changes fastest.
Arguments:
- queries: bfloat16 [4096, 32, 128], P(('dp', 'ctx'), 'head'), parts along dimension 0, may hold values from -112 to 112, as said below
- keys: bfloat16 [4096, 16, 128], P(('dp', 'ctx'), 'head'), parts along dimension 0, may hold values from -4 to 4, as said below
- values: bfloat16 [4096, 16, 128], P(('dp', 'ctx'), 'head'), parts along dimension 0, may hold values from -4 to 4
- out_grad: bfloat16 [4096, 32, 128], P(('dp', 'ctx'), 'head'), parts along dimension 0, may hold values from -4 to 4
- doc_lengths: int32 [32], P('dp'), parts along dimension 0, may hold values from 1 to 512, 2048 in all
Outputs:
- attended: bfloat16 [4096, 32, 128], P(('dp', 'ctx'), 'head'), parts along dimension 0
- query_grad: bfloat16 [4096, 32, 128], P(('dp', 'ctx'), 'head'), parts along dimension 0
- key_grad: bfloat16 [4096, 16, 128], P(('dp', 'ctx'), 'head'), parts along dimension 0
- value_grad: bfloat16 [4096, 16, 128], P(('dp', 'ctx'), 'head'), parts along dimension 0
There are 2 independent parts, one for each index of `dp`. A program takes and returns all parts, laid end to end along the dimension named above; each array names one. Nothing has to cross between parts.
Inputs may be any that keep to these rules, and one draw needn't show every extreme that they name: Entries of the queries lie in this range. Entries of the keys lie in this range. `doc_lengths`: the lengths sum to 2048; the longest document has exactly 512 tokens.
All inputs are finite; a program needn't handle non-finite values.
Results may differ from a plain program's by a relative error of at most 0.0055.
Values may be sent and summed in bfloat16 or wider, within the bound.
A program may use at most 192 MiB of HBM per device.

v0:
```python
import jax
import jax.numpy as jnp
from jax import lax
from jax.sharding import PartitionSpec as P

WINDOW = 1024
REACH = 4


SCALING = 168.0 ** (-0.5)


def shifted(array, axis, by):
    size = lax.axis_size(axis)
    pairs = [(i, i + by) for i in range(size) if 0 <= i + by < size]
    return lax.ppermute(array, axis, pairs)


def doc_index(positions, doc_lengths):
    ends = jnp.cumsum(doc_lengths)
    return jnp.sum((positions[:, None] >= ends[None, :]).astype(jnp.int32), axis=1)


def guarded(action, operands):
    return action(*operands)


def pair_products(left, right):
    return jnp.einsum("qhd,kd->hqk", left, right, preferred_element_type=jnp.float32)


def spread_back(weights_part, right):
    return jnp.einsum("hqk,kd->qhd", weights_part, right, preferred_element_type=jnp.float32)


def gather_rows(weights_part, left):
    return jnp.einsum("hqk,qhd->kd", weights_part, left, preferred_element_type=jnp.float32)


def body(queries, keys, values, out_grad, doc_lengths):
    rows = queries.shape[0]
    heads_local = queries.shape[1]
    kv_local = keys.shape[1]
    head_dim = keys.shape[2]
    group_size = heads_local // kv_local
    where_ctx = lax.axis_index("ctx")
    paired = jnp.stack((keys, values), 0)
    earlier = [shifted(paired, "ctx", distance) for distance in range(1, REACH + 1)]
    blocks_kv = [paired] + earlier
    query_pos = where_ctx * rows + jnp.arange(rows, dtype=jnp.int32)
    query_doc = doc_index(query_pos, doc_lengths)
    allowed_list = []
    live_list = []
    for distance in range(REACH + 1):
        key_pos = (where_ctx - distance) * rows + jnp.arange(rows, dtype=jnp.int32)
        key_doc = doc_index(key_pos, doc_lengths)
        gap = query_pos[:, None] - key_pos[None, :]
        allowed_list.append(
            (
                (gap >= 0)
                & (gap < WINDOW)
                & (key_pos[None, :] >= 0)
                & (query_doc[:, None] == key_doc[None, :])
            )[None]
        )
        live_list.append((where_ctx >= distance) & (query_doc[0] <= key_doc[rows - 1]))
    query_split = queries.reshape(rows, kv_local, group_size, head_dim)
    grad_split = out_grad.reshape(rows, kv_local, group_size, head_dim)
    out_shape = (rows, group_size, head_dim)
    spans = range(REACH + 1)
    out_groups = []
    qgrad_groups = []
    key_parts = [[] for d in spans]
    value_parts = [[] for d in spans]
    for group_index in range(kv_local):
        query_group = query_split[:, group_index]
        grad_group = grad_split[:, group_index]
        key_list = [block[0, :, group_index] for block in blocks_kv]
        value_list = [block[1, :, group_index] for block in blocks_kv]
        score_list = [SCALING * guarded(pair_products, (query_group, key_list[d])) for d in spans]
        maximum = score_list[0][:, :, :1] * 0.0 - jnp.inf
        for d in spans:
            maximum = jnp.maximum(
                maximum,
                jnp.max(jnp.where(allowed_list[d], score_list[d], -jnp.inf), axis=2, keepdims=True),
            )
        expo_list = [
            jnp.where(allowed_list[d], jnp.exp(score_list[d] - maximum), 0.0) for d in spans
        ]
        total = expo_list[0].sum(axis=2, keepdims=True)
        for d in range(1, REACH + 1):
            total = total + expo_list[d].sum(axis=2, keepdims=True)
        weight_list = [expo / total for expo in expo_list]
        rounded_list = [w.astype(jnp.bfloat16) for w in weight_list]
        attended = jnp.zeros(out_shape, jnp.float32)
        wgrad_list = []
        row_total = jnp.zeros_like(total)
        for d in spans:
            attended = attended + guarded(spread_back, (rounded_list[d], value_list[d]))
            wgrad = guarded(pair_products, (grad_group, value_list[d]))
            wgrad_list.append(wgrad)
            row_total = row_total + jnp.sum(weight_list[d] * wgrad, axis=2, keepdims=True)
        query_grad = jnp.zeros(out_shape, jnp.float32)
        for d in spans:
            grad_piece = (weight_list[d] * (wgrad_list[d] - row_total)).astype(jnp.bfloat16)
            query_grad = query_grad + guarded(spread_back, (grad_piece, key_list[d]))
            key_parts[d].append(SCALING * guarded(gather_rows, (grad_piece, query_group)))
            value_parts[d].append(guarded(gather_rows, (rounded_list[d], grad_group)))
        out_groups.append(attended.astype(jnp.bfloat16))
        qgrad_groups.append((SCALING * query_grad).astype(jnp.bfloat16))
    out_all = jnp.stack(out_groups, 1).reshape(rows, heads_local, head_dim)
    query_all = jnp.stack(qgrad_groups, 1).reshape(rows, heads_local, head_dim)
    partials = [
        jnp.stack((jnp.stack(key_parts[d], 1), jnp.stack(value_parts[d], 1)), 0) for d in spans
    ]
    summed = partials[0]
    for distance in range(1, REACH + 1):
        summed = summed + shifted(partials[distance], "ctx", -distance)
    return (out_all, query_all, summed[0].astype(jnp.bfloat16), summed[1].astype(jnp.bfloat16))


def solution(mesh):
    return jax.shard_map(
        body,
        mesh=mesh,
        in_specs=(
            P(("dp", "ctx"), "head", None),
            P(("dp", "ctx"), "head", None),
            P(("dp", "ctx"), "head", None),
            P(("dp", "ctx"), "head", None),
            P("dp"),
        ),
        out_specs=(
            P(("dp", "ctx"), "head", None),
            P(("dp", "ctx"), "head", None),
            P(("dp", "ctx"), "head", None),
            P(("dp", "ctx"), "head", None),
        ),
        check_vma=False,
    )
```

profile of v0, /device:TPU:15, one launch (start us, length us, event | category | flops | bytes accessed | tf_op | source)
XLA Modules:
  0.0 574.2 jit_solution(1857968334059134528)
XLA Ops:
  0.6 2.3 copy_bitcast_fusion
  2.9 2.3 pad_maximum_fusion.4
  5.2 5.2 collective-permute-start.3
  12.4 1.9 collective-permute-start.1
  14.3 1.9 collective-permute-start
  35.8 41.7 %collective-permute-done.3 = bf16[2,256,8,128]{3,1,2,0:T(8,128)(2,1)} collective-permute-done((bf16[2,256,8,128]{3,1,2,0:T(8,128)(2,1)}, bf16[2,256,8,128]{3,1,2,0:T(8,128)(2,1)}, u32[]{:S(2)}, u32[]{:S(2)}) %collective-permute-start.3) | collective-permute-done | bytes 1048608 | tf_op jit(solution)/shard_map/ppermute | solution.py:16
  78.5 21.4 %collective-permute-done.2 = bf16[2,256,8,128]{3,1,2,0:T(8,128)(2,1)} collective-permute-done((bf16[2,256,8,128]{3,1,2,0:T(8,128)(2,1)}, bf16[2,256,8,128]{3,1,2,0:T(8,128)(2,1)}, u32[]{:S(2)}, u32[]{:S(2)}) %collective-permute-start.2) | collective-permute-done | bytes 1048608 | tf_op jit(solution)/shard_map/ppermute | solution.py:16
  101.0 21.4 %collective-permute-done.1 = bf16[2,256,8,128]{3,1,2,0:T(8,128)(2,1)} collective-permute-done((bf16[2,256,8,128]{3,1,2,0:T(8,128)(2,1)}, bf16[2,256,8,128]{3,1,2,0:T(8,128)(2,1)}, u32[]{:S(2)}, u32[]{:S(2)}) %collective-permute-start.1) | collective-permute-done | bytes 1048608 | tf_op jit(solution)/shard_map/ppermute | solution.py:16
  123.5 21.4 %collective-permute-done = bf16[2,256,8,128]{3,1,2,0:T(8,128)(2,1)} collective-permute-done((bf16[2,256,8,128]{3,1,2,0:T(8,128)(2,1)}, bf16[2,256,8,128]{3,1,2,0:T(8,128)(2,1)}, u32[]{:S(2)}, u32[]{:S(2)}) %collective-permute-start) | collective-permute-done | bytes 1048608 | tf_op jit(solution)/shard_map/ppermute | solution.py:16
  174.5 2.0 convolution_bitcast_fusion.109
  201.5 2.3 multiply_reduce_fusion
  203.8 2.1 multiply_reduce_fusion.1
  207.5 2.3 multiply_reduce_fusion.3
  214.7 1.9 convolution_bitcast_fusion.94
  218.5 2.3 multiply_reduce_fusion.9
  233.6 2.3 multiply_reduce_fusion.5
  235.9 2.3 multiply_reduce_fusion.6
  238.1 2.2 multiply_reduce_fusion.7
  240.4 2.3 multiply_reduce_fusion.8
  353.1 2.1 collective-permute-start.4
  358.8 28.1 %collective-permute-done.7 = f32[2,256,8,128]{3,1,2,0:T(8,128)S(1)} collective-permute-done((f32[2,256,8,128]{3,1,2,0:T(8,128)S(1)}, f32[2,256,8,128]{3,1,2,0:T(8,128)S(1)}, u32[]{:S(2)}, u32[]{:S(2)}) %collective-permute-start.7) | collective-permute-done | bytes 2097184 | tf_op jit(solution)/shard_map/ppermute | solution.py:16
  386.9 24.7 %collective-permute-done.6 = f32[2,256,8,128]{3,1,2,0:T(8,128)S(1)} collective-permute-done((f32[2,256,8,128]{3,1,2,0:T(8,128)S(1)}, f32[2,256,8,128]{3,1,2,0:T(8,128)S(1)}, u32[]{:S(2)}, u32[]{:S(2)}) %collective-permute-start.6) | collective-permute-done | bytes 2097184 | tf_op jit(solution)/shard_map/ppermute | solution.py:16
  411.7 88.1 %collective-permute-done.5 = f32[2,256,8,128]{3,1,2,0:T(8,128)S(1)} collective-permute-done((f32[2,256,8,128]{3,1,2,0:T(8,128)S(1)}, f32[2,256,8,128]{3,1,2,0:T(8,128)S(1)}, u32[]{:S(2)}, u32[]{:S(2)}) %collective-permute-start.5) | collective-permute-done | bytes 2097184 | tf_op jit(solution)/shard_map/ppermute | solution.py:16
  499.8 71.0 %collective-permute-done.4 = f32[2,256,8,128]{3,1,2,0:T(8,128)S(1)} collective-permute-done((f32[2,256,8,128]{3,1,2,0:T(8,128)S(1)}, f32[2,256,8,128]{3,1,2,0:T(8,128)S(1)}, u32[]{:S(2)}, u32[]{:S(2)}) %collective-permute-start.4) | collective-permute-done | bytes 2097184 | tf_op jit(solution)/shard_map/ppermute | solution.py:16
  (361 shorter events, 215.7 us)
Async XLA Ops:
  0.6 15.7 %copy-start.11 = (bf16[256,16,128]{2,1,0:T(8,128)(2,1)S(1)}, bf16[256,16,128]{2,1,0:T(8,128)(2,1)}, u32[]{:S(2)}) copy-start(bf16[256,16,128]{2,1,0:T(8,128)(2,1)} %param.5) | copy-start | bytes 3145732
  2.9 17.3 %copy-start.3 = (bf16[1,256,8,128]{3,1,2,0:T(8,128)(2,1)}, bf16[1,256,8,128]{3,1,2,0:T(8,128)(2,1)S(1)}, u32[]{:S(2)}) copy-start(bf16[1,256,8,128]{3,1,2,0:T(8,128)(2,1)S(1)} %get-tuple-element.243) | copy-start | bytes 1572868
  5.2 72.3 %collective-permute-start.3 = (bf16[2,256,8,128]{3,1,2,0:T(8,128)(2,1)}, bf16[2,256,8,128]{3,1,2,0:T(8,128)(2,1)}, u32[]{:S(2)}, u32[]{:S(2)}) collective-permute-start(bf16[2,256,8,128]{3,1,2,0:T(8,128)(2,1)} %pad_maximum_fusion.4), channel_id=1, source_target_pairs={{0,8},{2,10},{4,12},{6,14},{1,9},{3,11},{5,13},{7,15},{16,24},{18,... | collective-permute-start | bytes 3145736 | tf_op jit(solution)/shard_map/ppermute | solution.py:16
  10.5 89.5 %collective-permute-start.2 = (bf16[2,256,8,128]{3,1,2,0:T(8,128)(2,1)}, bf16[2,256,8,128]{3,1,2,0:T(8,128)(2,1)}, u32[]{:S(2)}, u32[]{:S(2)}) collective-permute-start(bf16[2,256,8,128]{3,1,2,0:T(8,128)(2,1)} %pad_maximum_fusion.4), channel_id=1, source_target_pairs={{0,6},{2,8},{4,10},{6,12},{8,14},{1,7},{3,9},{5,11},{7,13},{9,15},... | collective-permute-start | bytes 3145736 | tf_op jit(solution)/shard_map/ppermute | solution.py:16
  12.4 110.0 %collective-permute-start.1 = (bf16[2,256,8,128]{3,1,2,0:T(8,128)(2,1)}, bf16[2,256,8,128]{3,1,2,0:T(8,128)(2,1)}, u32[]{:S(2)}, u32[]{:S(2)}) collective-permute-start(bf16[2,256,8,128]{3,1,2,0:T(8,128)(2,1)} %pad_maximum_fusion.4), channel_id=1, source_target_pairs={{0,4},{2,6},{4,8},{6,10},{8,12},{10,14},{1,5},{3,7},{5,9},{7,11},{... | collective-permute-start | bytes 3145736 | tf_op jit(solution)/shard_map/ppermute | solution.py:16
  14.3 130.6 %collective-permute-start = (bf16[2,256,8,128]{3,1,2,0:T(8,128)(2,1)}, bf16[2,256,8,128]{3,1,2,0:T(8,128)(2,1)}, u32[]{:S(2)}, u32[]{:S(2)}) collective-permute-start(bf16[2,256,8,128]{3,1,2,0:T(8,128)(2,1)} %pad_maximum_fusion.4), channel_id=1, source_target_pairs={{0,2},{2,4},{4,6},{6,8},{8,10},{10,12},{12,14},{1,3},{3,5},{5,7},{... | collective-permute-start | bytes 3145736 | tf_op jit(solution)/shard_map/ppermute | solution.py:16
  16.6 4.6 copy-start.12
  21.5 9.4 %copy-start.20 = (s32[16]{0:T(128)S(1)}, s32[16]{0:T(128)}, u32[]{:S(2)}) copy-start(s32[16]{0:T(128)} %param.9) | copy-start | bytes 196
  147.1 3.4 copy-start.1
  163.3 2.5 copy-start
  163.3 2.5 copy-start.2
  174.4 4.0 copy-start.5
  174.4 4.0 copy-start.6
  174.5 4.0 copy-start.8
  174.5 4.0 copy-start.9
  174.5 4.0 copy-start.10
  214.7 3.8 copy-start.7
  267.9 2.5 copy-start.22
  271.7 2.5 copy-start.26
  272.9 2.5 copy-start.27
  337.4 49.6 %collective-permute-start.7 = (f32[2,256,8,128]{3,1,2,0:T(8,128)S(1)}, f32[2,256,8,128]{3,1,2,0:T(8,128)S(1)}, u32[]{:S(2)}, u32[]{:S(2)}) collective-permute-start(f32[2,256,8,128]{3,1,2,0:T(8,128)S(1)} %pad_maximum_fusion.3), channel_id=1, source_target_pairs={{8,0},{10,2},{12,4},{14,6},{9,1},{11,3},{13,5},{15,7},{24,16},{26,... | collective-permute-start | bytes 6291464 | tf_op jit(solution)/shard_map/ppermute | solution.py:16
  342.2 69.5 %collective-permute-start.6 = (f32[2,256,8,128]{3,1,2,0:T(8,128)S(1)}, f32[2,256,8,128]{3,1,2,0:T(8,128)S(1)}, u32[]{:S(2)}, u32[]{:S(2)}) collective-permute-start(f32[2,256,8,128]{3,1,2,0:T(8,128)S(1)} %pad_maximum_fusion.2), channel_id=1, source_target_pairs={{6,0},{8,2},{10,4},{12,6},{14,8},{7,1},{9,3},{11,5},{13,7},{15,9},... | collective-permute-start | bytes 6291464 | tf_op jit(solution)/shard_map/ppermute | solution.py:16
  347.7 152.1 %collective-permute-start.5 = (f32[2,256,8,128]{3,1,2,0:T(8,128)S(1)}, f32[2,256,8,128]{3,1,2,0:T(8,128)S(1)}, u32[]{:S(2)}, u32[]{:S(2)}) collective-permute-start(f32[2,256,8,128]{3,1,2,0:T(8,128)S(1)} %pad_maximum_fusion.1), channel_id=1, source_target_pairs={{4,0},{6,2},{8,4},{10,6},{12,8},{14,10},{5,1},{7,3},{9,5},{11,7},{... | collective-permute-start | bytes 6291464 | tf_op jit(solution)/shard_map/ppermute | solution.py:16
  353.1 217.7 %collective-permute-start.4 = (f32[2,256,8,128]{3,1,2,0:T(8,128)S(1)}, f32[2,256,8,128]{3,1,2,0:T(8,128)S(1)}, u32[]{:S(2)}, u32[]{:S(2)}) collective-permute-start(f32[2,256,8,128]{3,1,2,0:T(8,128)S(1)} %pad_maximum_fusion), channel_id=1, source_target_pairs={{2,0},{4,2},{6,4},{8,6},{10,8},{12,10},{14,12},{3,1},{5,3},{7,5},{... | collective-permute-start | bytes 6291464 | tf_op jit(solution)/shard_map/ppermute | solution.py:16
  (12 other events, 21.7 us)
where the time goes:
time: 584 us; the launch traced here: 574 us
  waiting for transfers between devices  318 us (54%)
  matrix products  210 us (36%)
  starting transfers between devices  18.2 us (3%)
  other arithmetic  15 us (3%)
  local copies, waits for them, and re-layouts  10.4 us (2%)
    ppermute x8, waiting for transfers between devices, shifted(): return lax.ppermute(array, axis, pairs)  318 us
    dot_general x80, matrix products, pair_products(): jnp.einsum('qhd,kd->hqk', left, right, preferred_element_type=jnp.float32)  99.9 us
    dot_general x80, matrix products, spread_back(): jnp.einsum('hqk,kd->qhd', weights_part, right, preferred_element_type=jnp...  91.4 us
    dot_general x80, matrix products, gather_rows(): jnp.einsum('hqk,qhd->kd', weights_part, left, preferred_element_type=jnp....  18.6 us
    ppermute x8, starting transfers between devices, shifted(): return lax.ppermute(array, axis, pairs)  18.2 us
  transfers between devices with their start and end apart: 8, of which 8 were waited for; matrix products, arithmetic and copies ran while one was open for 6% of the time, Pallas kernels for 0%

commit v1 on v0

v1 whole, which is shorter than its diff:
```python
import functools

import jax
import jax.numpy as jnp
from jax import lax
from jax.experimental import pallas as pl
from jax.experimental.pallas import tpu as pltpu
from jax.sharding import PartitionSpec as P

WINDOW = 1024
SCALING = 168.0 ** (-0.5)
LOG2E = 1.4426950408889634
MASKED = -1e30
MESH = pl.DeviceIdType.MESH
F32 = jnp.float32
BF16 = jnp.bfloat16


def kernel(
    size, reach, doc_ref, q_ref, g_ref, k_ref, v_ref,
    out_ref, dq_ref, dk_ref, dv_ref,
    k_all, v_all, k_own, v_own, k_part, v_part, k_back, v_back, bias,
    kv_send, kv_recv, grad_send, grad_recv,
):
    groups, rows, dim = k_ref.shape
    span = (reach + 1) * rows
    me = lax.axis_index("ctx")
    distances = range(1, reach + 1)

    def slot(d):
        return pl.ds((reach - d) * rows, rows)

    def outward(d, g, which):
        src, dst = ((k_ref, k_all), (v_ref, v_all))[which]
        return pltpu.make_async_remote_copy(
            src_ref=src.at[g],
            dst_ref=dst.at[g, slot(d)],
            send_sem=kv_send.at[d - 1, which, g],
            recv_sem=kv_recv.at[d - 1, which, g],
            device_id={"ctx": me + d},
            device_id_type=MESH,
        )

    def backward(d, g, which):
        src, dst = ((k_part, k_back), (v_part, v_back))[which]
        return pltpu.make_async_remote_copy(
            src_ref=src.at[d - 1, g],
            dst_ref=dst.at[d - 1, g],
            send_sem=grad_send.at[d - 1, which, g],
            recv_sem=grad_recv.at[d - 1, which, g],
            device_id={"ctx": me - d},
            device_id_type=MESH,
        )

    barrier = pltpu.get_barrier_semaphore()
    for d in distances:
        @pl.when(me + d < size)
        def _():
            pl.semaphore_signal(barrier, inc=1, device_id={"ctx": me + d}, device_id_type=MESH)

        @pl.when(me >= d)
        def _():
            pl.semaphore_signal(barrier, inc=1, device_id={"ctx": me - d}, device_id_type=MESH)

    peers = jnp.minimum(me, reach) + jnp.minimum(size - 1 - me, reach)
    pl.semaphore_wait(barrier, peers)

    @pl.loop(0, groups)
    def _(g):
        for d in distances:
            @pl.when(me + d < size)
            def _():
                for which in range(2):
                    outward(d, g, which).start()

    lane = lax.broadcasted_iota(jnp.int32, (1, rows), 1)
    position = me * rows + lane
    first = jnp.maximum(position - (WINDOW - 1), 0)
    end = jnp.int32(0)
    for n in range(doc_ref.shape[0]):
        end = end + doc_ref[n]
        first = jnp.maximum(first, jnp.where(position >= end, end, 0))
    first = first - (me - reach) * rows
    at = lax.broadcasted_iota(jnp.int32, (span, rows), 0)
    seen = (at >= first) & (at <= lane + reach * rows)
    mask = jnp.where(seen, 0.0, MASKED).astype(F32)
    bias[:, :rows] = mask
    bias[:, rows:] = mask

    k_all[:, slot(0), :] = k_ref[...]
    v_all[:, slot(0), :] = v_ref[...]
    for d in distances:
        @pl.when(me < d)
        def _():
            k_all[:, slot(d), :] = jnp.zeros((groups, rows, dim), BF16)
            v_all[:, slot(d), :] = jnp.zeros((groups, rows, dim), BF16)

    def across(left, right):
        return lax.dot_general(left, right, (((1,), (1,)), ((), ())), preferred_element_type=F32)

    def product(left, right):
        return jnp.dot(left, right, preferred_element_type=F32)

    def flipped(array):
        return array.astype(F32).T.astype(BF16)

    @pl.loop(0, groups)
    def _(g):
        for d in distances:
            @pl.when(me >= d)
            def _():
                for which in range(2):
                    outward(d, g, which).wait_recv()

        query, grad, key, value = q_ref[g], g_ref[g], k_all[g], v_all[g]
        scores = across(key, query) * (SCALING * LOG2E) + bias[...]
        expo = jnp.exp2(scores - jnp.max(scores, axis=0, keepdims=True))
        weights = expo * (1.0 / jnp.sum(expo, axis=0, keepdims=True))
        rounded = weights.astype(BF16)
        weight_grad = across(value, grad)
        row_total = jnp.sum(weights * weight_grad, axis=0, keepdims=True)
        score_grad = (weights * (weight_grad - row_total)).astype(BF16)
        key_grad = product(score_grad, query) * SCALING
        value_grad = product(rounded, grad)
        k_own[g] = key_grad[reach * rows:]
        v_own[g] = value_grad[reach * rows:]
        for d in distances:
            low = (reach - d) * rows
            k_part[d - 1, g] = key_grad[low:low + rows].astype(BF16)
            v_part[d - 1, g] = value_grad[low:low + rows].astype(BF16)

            @pl.when(me >= d)
            def _():
                for which in range(2):
                    backward(d, g, which).start()

        out_ref[g] = product(flipped(value), rounded).T.astype(BF16)
        dq_ref[g] = (product(flipped(key), score_grad) * SCALING).T.astype(BF16)

    @pl.loop(0, groups)
    def _(g):
        for d in distances:
            @pl.when(me + d < size)
            def _():
                for which in range(2):
                    backward(d, g, which).wait_recv()
                k_own[g] += k_back[d - 1, g].astype(F32)
                v_own[g] += v_back[d - 1, g].astype(F32)

        dk_ref[g] = k_own[g].astype(BF16)
        dv_ref[g] = v_own[g].astype(BF16)

    @pl.loop(0, groups)
    def _(g):
        for d in distances:
            @pl.when(me + d < size)
            def _():
                for which in range(2):
                    outward(d, g, which).wait_send()

            @pl.when(me >= d)
            def _():
                for which in range(2):
                    backward(d, g, which).wait_send()


def body(queries, keys, values, out_grad, doc_lengths):
    rows, heads, dim = queries.shape
    groups = keys.shape[1]
    per = heads // groups
    size = lax.axis_size("ctx")
    reach = min(WINDOW, rows * size // 4) // rows
    span = (reach + 1) * rows

    def split(array):
        return array.reshape(rows, groups, per, dim).transpose(1, 2, 0, 3).reshape(groups, per * rows, dim)

    def joined(array):
        return array.reshape(groups, per, rows, dim).transpose(2, 0, 1, 3).reshape(rows, heads, dim)

    vmem = pl.BlockSpec(memory_space=pltpu.VMEM)
    dma = pltpu.SemaphoreType.DMA((reach, 2, groups))
    wide = jax.ShapeDtypeStruct((groups, per * rows, dim), BF16)
    narrow = jax.ShapeDtypeStruct((groups, rows, dim), BF16)
    out, dq, dk, dv = pl.pallas_call(
        functools.partial(kernel, size, reach),
        out_shape=(wide, wide, narrow, narrow),
        in_specs=[pl.BlockSpec(memory_space=pltpu.SMEM)] + [vmem] * 4,
        out_specs=(vmem,) * 4,
        scratch_shapes=[
            pltpu.VMEM((groups, span, dim), BF16),
            pltpu.VMEM((groups, span, dim), BF16),
            pltpu.VMEM((groups, rows, dim), F32),
            pltpu.VMEM((groups, rows, dim), F32),
            pltpu.VMEM((reach, groups, rows, dim), BF16),
            pltpu.VMEM((reach, groups, rows, dim), BF16),
            pltpu.VMEM((reach, groups, rows, dim), BF16),
            pltpu.VMEM((reach, groups, rows, dim), BF16),
            pltpu.VMEM((span, per * rows), F32),
            dma, dma, dma, dma,
        ],
        compiler_params=pltpu.CompilerParams(
            collective_id=0, has_side_effects=True, vmem_limit_bytes=56 * 2**20
        ),
    )(doc_lengths, split(queries), split(out_grad), keys.transpose(1, 0, 2), values.transpose(1, 0, 2))
    return joined(out), joined(dq), dk.transpose(1, 0, 2), dv.transpose(1, 0, 2)


def solution(mesh):
    spec = P(("dp", "ctx"), "head", None)
    return jax.shard_map(
        body,
        mesh=mesh,
        in_specs=(spec, spec, spec, spec, P("dp")),
        out_specs=(spec, spec, spec, spec),
        check_vma=False,
    )
```

time: 584 us -> 74.5 us (0.13)
  the two profiles are of different devices: /device:TPU:15 before, /device:TPU:0 now
where the time goes in v1:
time: 74.5 us; the launch traced here: 74.3 us
  Pallas kernels  60.9 us (82%)
  local copies, waits for them, and re-layouts  12.7 us (17%)
    pallas_call x1, Pallas kernels, body(): pl.pallas_call(functools.partial(kernel, size, reach), out_shape=(wide, w...  60.9 us
    transpose x2, local copies, waits for them, and re-layouts, joined(): array.reshape(groups, per, rows, dim).transpose(2, 0, 1, 3)  5.41 us
    reshape x2, local copies, waits for them, and re-layouts, split(): array.reshape(rows, groups, per, dim).transpose(1, 2, 0, 3)  3.8 us
    unnamed x14, local copies, waits for them, and re-layouts  2.29 us

profile of v1, /device:TPU:0, one launch (start us, length us, event | category | flops | bytes accessed | tf_op | source)
XLA Modules:
  0.0 74.3 jit_solution(15787373314529634855)
XLA Ops:
  0.6 0.0 copy-start
  0.6 2.6 %copy.9 = bf16[256,8,2,128]{3,0,2,1:T(8,128)(2,1)} copy(bf16[256,8,2,128]{3,2,1,0:T(2,128)(2,1)} %bitcast.24) | data formatting | bytes 2097152 | tf_op jit(solution)/shard_map/reshape | solution.py:176
  3.2 0.0 copy-done
  3.2 0.0 copy-start.4
  3.2 0.0 copy-start.5
  3.2 1.2 %copy.10 = bf16[256,8,2,128]{3,0,2,1:T(8,128)(2,1)} copy(bf16[256,8,2,128]{3,2,1,0:T(2,128)(2,1)S(1)} %bitcast.25) | data formatting | bytes 2097152 | tf_op jit(solution)/shard_map/reshape | solution.py:176
  4.4 0.0 copy-done.4
  4.4 0.0 copy-done.5
  4.5 1.2 %copy_bitcast_fusion = (bf16[8,256,128]{2,1,0:T(8,128)(2,1)}, bf16[8,256,128]{2,1,0:T(8,128)(2,1)}) fusion(bf16[256,8,128]{2,1,0:T(8,128)(2,1)S(1)} %copy-done.4, bf16[256,8,128]{2,1,0:T(8,128)(2,1)S(1)} %copy-done.5), kind=kLoop, calls=%fused_computation | loop fusion | bytes 2097152 | tf_op jit(solution)/shard_map/transpose | solution.py:205
  5.6 60.9 %shard_map.84 = (bf16[8,512,128]{2,1,0:T(8,128)(2,1)}, bf16[8,512,128]{2,1,0:T(8,128)(2,1)}, bf16[8,256,128]{2,1,0:T(8,128)(2,1)}, bf16[8,256,128]{2,1,0:T(8,128)(2,1)}) custom-call(s32[16]{0:T(128)} %doc_ref.1, bf16[8,512,128]{2,1,0:T(8,128)(2,1)} %bitcast.22, bf16[8,512,128]{2,1,0:T(8,128)(2,1)} %bitcast.23, bf16[8,256,128]{2,1,0:T(8,128)(2,1)} %get-tuple-element.17.k_ref, ...), custom_call_target="tpu_custom_call" | custom-call | tf_op jit(solution)/shard_map/pallas_call | solution.py:185
  66.6 0.0 copy-start.1
  66.6 3.4 %copy.13 = bf16[256,8,2,128]{3,2,1,0:T(2,128)(2,1)} copy(bf16[256,8,2,128]{3,0,2,1:T(8,128)(2,1)} %bitcast.29) | data formatting | bytes 2097152 | tf_op jit(solution)/shard_map/transpose | solution.py:179
  69.9 0.0 copy-done.1
  69.9 0.0 copy-start.3
  69.9 2.0 %copy.14 = bf16[256,8,2,128]{3,2,1,0:T(2,128)(2,1)} copy(bf16[256,8,2,128]{3,0,2,1:T(8,128)(2,1)S(1)} %bitcast.28) | data formatting | bytes 2097152 | tf_op jit(solution)/shard_map/transpose | solution.py:179
  72.0 0.0 copy-done.3
  72.0 0.0 copy-start.2
  72.0 1.1 %copy.15 = bf16[256,8,128]{2,1,0:T(8,128)(2,1)} copy(bf16[256,8,128]{2,0,1:T(8,128)(2,1)S(1)} %bitcast.31) | data formatting | bytes 1048576
  73.1 0.0 copy-done.2
  73.1 1.1 %copy.16 = bf16[256,8,128]{2,1,0:T(8,128)(2,1)} copy(bf16[256,8,128]{2,0,1:T(8,128)(2,1)S(1)} %bitcast.30) | data formatting | bytes 1048576
Async XLA Ops:
  0.6 2.6 %copy-start = (bf16[256,16,128]{2,1,0:T(8,128)(2,1)S(1)}, bf16[256,16,128]{2,1,0:T(8,128)(2,1)}, u32[]{:S(2)}) copy-start(bf16[256,16,128]{2,1,0:T(8,128)(2,1)} %param.8) | copy-start | bytes 3145732
  3.2 1.2 %copy-start.4 = (bf16[256,8,128]{2,1,0:T(8,128)(2,1)S(1)}, bf16[256,8,128]{2,1,0:T(8,128)(2,1)}, u32[]{:S(2)}) copy-start(bf16[256,8,128]{2,1,0:T(8,128)(2,1)} %param.7) | copy-start | bytes 1572868
  3.2 1.2 %copy-start.5 = (bf16[256,8,128]{2,1,0:T(8,128)(2,1)S(1)}, bf16[256,8,128]{2,1,0:T(8,128)(2,1)}, u32[]{:S(2)}) copy-start(bf16[256,8,128]{2,1,0:T(8,128)(2,1)} %param.6) | copy-start | bytes 1572868
  66.6 3.4 %copy-start.1 = (bf16[8,512,128]{2,1,0:T(8,128)(2,1)S(1)}, bf16[8,512,128]{2,1,0:T(8,128)(2,1)}, u32[]{:S(2)}) copy-start(bf16[8,512,128]{2,1,0:T(8,128)(2,1)} %get-tuple-element.9) | copy-start | bytes 3145732
  69.9 2.1 %copy-start.3 = (bf16[8,256,128]{2,1,0:T(8,128)(2,1)S(1)}, bf16[8,256,128]{2,1,0:T(8,128)(2,1)}, u32[]{:S(2)}) copy-start(bf16[8,256,128]{2,1,0:T(8,128)(2,1)} %get-tuple-element.10) | copy-start | bytes 1572868
  72.0 1.1 %copy-start.2 = (bf16[8,256,128]{2,1,0:T(8,128)(2,1)S(1)}, bf16[8,256,128]{2,1,0:T(8,128)(2,1)}, u32[]{:S(2)}) copy-start(bf16[8,256,128]{2,1,0:T(8,128)(2,1)} %get-tuple-element.11) | copy-start | bytes 1572868

commit v2 on v1

v2 whole, which is shorter than its diff:
```python
import functools

import jax
import jax.numpy as jnp
from jax import lax
from jax.experimental import pallas as pl
from jax.experimental.pallas import tpu as pltpu
from jax.sharding import PartitionSpec as P

WINDOW = 1024
SCALING = 168.0 ** (-0.5)
LOG2E = 1.4426950408889634
MASKED = -1e30
LAG = 2
MESH = pl.DeviceIdType.MESH
F32 = jnp.float32
BF16 = jnp.bfloat16


def kernel(
    size, reach, doc_ref, q_ref, g_ref, k_ref, v_ref,
    out_ref, dq_ref, dk_ref, dv_ref,
    q_wide, g_wide, k_wide, v_wide, out_wide, dq_wide, dk_wide, dv_wide,
    kv_all, part, back, relay, bias,
    kv_send, kv_recv, grad_send, grad_recv, relay_recv, pass_send,
):
    rows, groups, dim = k_ref.shape
    heads = q_ref.shape[1]
    per = heads // groups
    span = (reach + 1) * rows
    me = lax.axis_index("ctx")
    plane, spot = me // reach, me % reach
    planes = size // reach
    distances = range(1, reach + 1)
    near = range(1, reach)

    def slot(d):
        return pl.ds((reach - d) * rows, rows)

    def remote(src, dst, send, recv, to):
        return pltpu.make_async_remote_copy(
            src_ref=src, dst_ref=dst, send_sem=send, recv_sem=recv,
            device_id={"ctx": to}, device_id_type=MESH,
        )

    def outward(d, g):
        return remote(
            kv_all.at[g, :, slot(0)], kv_all.at[g, :, slot(d)],
            kv_send.at[d - 1, g], kv_recv.at[d - 1, g], me + d,
        )

    def passed(d, g):
        return remote(
            kv_all.at[g, :, slot(reach)], kv_all.at[g, :, slot(d)],
            pass_send.at[d - 1, g], kv_recv.at[d - 1, g], me - (reach - d),
        )

    def homeward(d, g):
        return remote(
            part.at[d - 1, g], back.at[d - 1, g],
            grad_send.at[d - 1, g], grad_recv.at[d - 1, g], me - d,
        )

    def relayed(d, g):
        return remote(
            part.at[d - 1, g], relay.at[d - 1, g],
            grad_send.at[d - 1, g], relay_recv.at[d - 1, g], me + (reach - d),
        )

    barrier = pltpu.get_barrier_semaphore()

    def greet(to):
        pl.semaphore_signal(barrier, inc=1, device_id={"ctx": to}, device_id_type=MESH)

    for o in near:
        greet(plane * reach + (spot + o) % reach)

    @pl.when(plane > 0)
    def _():
        greet(me - reach)

    @pl.when(plane < planes - 1)
    def _():
        greet(me + reach)

    k_wide[...] = k_ref[...].astype(F32).reshape(rows * groups, dim)
    v_wide[...] = v_ref[...].astype(F32).reshape(rows * groups, dim)
    peers = (reach - 1) + jnp.minimum(plane, 1) + jnp.minimum(planes - 1 - plane, 1)
    pl.semaphore_wait(barrier, peers)

    @pl.loop(0, groups)
    def _(g):
        kv_all[g, 0, slot(0), :] = k_wide[pl.ds(g, rows, stride=groups), :].astype(BF16)
        kv_all[g, 1, slot(0), :] = v_wide[pl.ds(g, rows, stride=groups), :].astype(BF16)

        @pl.when(plane < planes - 1)
        def _():
            outward(reach, g).start()

        for d in near:
            @pl.when(spot + d < reach)
            def _():
                outward(d, g).start()

    q_wide[...] = q_ref[...].astype(F32).reshape(rows * heads, dim)
    g_wide[...] = g_ref[...].astype(F32).reshape(rows * heads, dim)

    lane = lax.broadcasted_iota(jnp.int32, (1, rows), 1)
    position = me * rows + lane
    first = jnp.maximum(position - (WINDOW - 1), 0)
    end = jnp.int32(0)
    for n in range(doc_ref.shape[0]):
        end = end + doc_ref[n]
        first = jnp.maximum(first, jnp.where(position >= end, end, 0))
    first = first - (me - reach) * rows
    at = lax.broadcasted_iota(jnp.int32, (span, rows), 0)
    seen = (at >= first) & (at <= lane + reach * rows)
    mask = jnp.where(seen, 0.0, MASKED).astype(F32)
    for n in range(per):
        bias[:, n * rows:(n + 1) * rows] = mask

    for d in distances:
        @pl.when(me < d)
        def _():
            kv_all[:, :, slot(d), :] = jnp.zeros((groups, 2, rows, dim), BF16)

    def across(left, right):
        return lax.dot_general(left, right, (((1,), (1,)), ((), ())), preferred_element_type=F32)

    def product(left, right):
        return jnp.dot(left, right, preferred_element_type=F32)

    def flipped(array):
        return array.astype(F32).T.astype(BF16)

    def head_rows(wide, g):
        return jnp.concatenate(
            [wide[pl.ds(g * per + n, rows, stride=heads), :] for n in range(per)], 0
        ).astype(BF16)

    def store_heads(wide, g, array):
        for n in range(per):
            wide[pl.ds(g * per + n, rows, stride=heads), :] = array[n * rows:(n + 1) * rows]

    def send_far(g):
        @pl.when(plane > 0)
        def _():
            for d in near:
                @pl.when(spot >= reach - d)
                def _():
                    remote(
                        part.at[d - 1, g], relay.at[d - 1, g],
                        grad_send.at[d - 1, g], relay_recv.at[d - 1, g], me - (reach - d),
                    ).wait_recv()
                    total = part[reach - 1, g].astype(F32) + relay[d - 1, g].astype(F32)
                    part[reach - 1, g] = total.astype(BF16)
            homeward(reach, g).start()

    @pl.loop(0, groups)
    def _(g):
        @pl.when(plane > 0)
        def _():
            outward(reach, g).wait_recv()
            for d in near:
                @pl.when(spot >= reach - d)
                def _():
                    passed(d, g).start()

        for d in near:
            @pl.when(me >= d)
            def _():
                outward(d, g).wait_recv()

        query, grad = head_rows(q_wide, g), head_rows(g_wide, g)
        key, value = kv_all[g, 0], kv_all[g, 1]
        scores = across(key, query) * (SCALING * LOG2E) + bias[...]
        expo = jnp.exp2(scores - jnp.max(scores, axis=0, keepdims=True))
        weights = expo * (1.0 / jnp.sum(expo, axis=0, keepdims=True))
        rounded = weights.astype(BF16)
        weight_grad = across(value, grad)
        row_total = jnp.sum(weights * weight_grad, axis=0, keepdims=True)
        score_grad = (weights * (weight_grad - row_total)).astype(BF16)
        key_grad = product(score_grad, query) * SCALING
        value_grad = product(rounded, grad)
        dk_wide[pl.ds(g, rows, stride=groups), :] = key_grad[reach * rows:]
        dv_wide[pl.ds(g, rows, stride=groups), :] = value_grad[reach * rows:]
        for d in distances:
            low = (reach - d) * rows
            part[d - 1, g, 0] = key_grad[low:low + rows].astype(BF16)
            part[d - 1, g, 1] = value_grad[low:low + rows].astype(BF16)
        for d in near:
            @pl.when(spot >= d)
            def _():
                homeward(d, g).start()

            @pl.when((spot < d) & (plane > 0))
            def _():
                relayed(d, g).start()

        store_heads(out_wide, g, product(flipped(value), rounded).T)
        store_heads(dq_wide, g, (product(flipped(key), score_grad) * SCALING).T)

        @pl.when(g >= LAG)
        def _():
            send_far(g - LAG)

    @pl.loop(groups - LAG, groups)
    def _(g):
        send_far(g)

    out_ref[...] = out_wide[...].reshape(rows, heads, dim).astype(BF16)
    dq_ref[...] = dq_wide[...].reshape(rows, heads, dim).astype(BF16)

    def add_back(d, g):
        homeward(d, g).wait_recv()
        dk_wide[pl.ds(g, rows, stride=groups), :] += back[d - 1, g, 0].astype(F32)
        dv_wide[pl.ds(g, rows, stride=groups), :] += back[d - 1, g, 1].astype(F32)

    @pl.loop(0, groups)
    def _(g):
        for d in near:
            @pl.when(spot + d < reach)
            def _():
                add_back(d, g)

        @pl.when(plane < planes - 1)
        def _():
            add_back(reach, g)

    dk_ref[...] = dk_wide[...].reshape(rows, groups, dim).astype(BF16)
    dv_ref[...] = dv_wide[...].reshape(rows, groups, dim).astype(BF16)

    @pl.loop(0, groups)
    def _(g):
        @pl.when(plane < planes - 1)
        def _():
            outward(reach, g).wait_send()

        @pl.when(plane > 0)
        def _():
            homeward(reach, g).wait_send()

        for d in near:
            @pl.when(spot + d < reach)
            def _():
                outward(d, g).wait_send()

            @pl.when((plane > 0) & (spot >= reach - d))
            def _():
                passed(d, g).wait_send()

            @pl.when(me >= d)
            def _():
                homeward(d, g).wait_send()


def body(queries, keys, values, out_grad, doc_lengths):
    rows, heads, dim = queries.shape
    groups = keys.shape[1]
    size = lax.axis_size("ctx")
    reach = min(WINDOW, rows * size // 4) // rows
    span = (reach + 1) * rows
    vmem = pl.BlockSpec(memory_space=pltpu.VMEM)
    dma = pltpu.SemaphoreType.DMA((reach, groups))
    wide = jax.ShapeDtypeStruct(queries.shape, BF16)
    narrow = jax.ShapeDtypeStruct(keys.shape, BF16)
    shares = pltpu.VMEM((reach, groups, 2, rows, dim), BF16)
    return pl.pallas_call(
        functools.partial(kernel, size, reach),
        out_shape=(wide, wide, narrow, narrow),
        in_specs=[pl.BlockSpec(memory_space=pltpu.SMEM)] + [vmem] * 4,
        out_specs=(vmem,) * 4,
        scratch_shapes=[
            pltpu.VMEM((rows * heads, dim), F32),
            pltpu.VMEM((rows * heads, dim), F32),
            pltpu.VMEM((rows * groups, dim), F32),
            pltpu.VMEM((rows * groups, dim), F32),
            pltpu.VMEM((rows * heads, dim), F32),
            pltpu.VMEM((rows * heads, dim), F32),
            pltpu.VMEM((rows * groups, dim), F32),
            pltpu.VMEM((rows * groups, dim), F32),
            pltpu.VMEM((groups, 2, span, dim), BF16),
            shares, shares, shares,
            pltpu.VMEM((span, heads // groups * rows), F32),
            dma, dma, dma, dma, dma, dma,
        ],
        compiler_params=pltpu.CompilerParams(
            collective_id=0, has_side_effects=True, vmem_limit_bytes=58 * 2**20
        ),
    )(doc_lengths, queries, out_grad, keys, values)


def solution(mesh):
    spec = P(("dp", "ctx"), "head", None)
    return jax.shard_map(
        body,
        mesh=mesh,
        in_specs=(spec, spec, spec, spec, P("dp")),
        out_specs=(spec, spec, spec, spec),
        check_vma=False,
    )
```

time: 74.5 us -> 79.4 us (1.066)
  Pallas kernels: 60.9 us -> 72.6 us
  local copies, waits for them, and re-layouts: 12.7 us -> 5.88 us
    pallas_call x1, Pallas kernels: 60.9 us -> 72.6 us  [body(): pl.pallas_call(functools.partial(kernel, size, reach), out_shape=(wide, w...]
    transpose x3 -> x0, local copies, waits for them, and re-layouts: 6.56 us -> none  [the longest x2 5.41 us: joined(): array.reshape(groups, per, rows, dim).transpose(2, 0, 1, 3)]
    reshape x2 -> x0, local copies, waits for them, and re-layouts: 3.8 us -> none  [split(): array.reshape(rows, groups, per, dim).transpose(1, 2, 0, 3)]
    unnamed x14 -> x10, local copies, waits for them, and re-layouts: 2.29 us -> 5.88 us
where the time goes in v2:
time: 79.4 us; the launch traced here: 79.2 us
  Pallas kernels  72.6 us (91%)
  local copies, waits for them, and re-layouts  5.88 us (7%)
    pallas_call x1, Pallas kernels, body(): pl.pallas_call(functools.partial(kernel, size, reach), out_shape=(wide, w...  72.6 us
    unnamed x10, local copies, waits for them, and re-layouts  5.88 us

profile of v2, /device:TPU:0, one launch (start us, length us, event | category | flops | bytes accessed | tf_op | source)
XLA Modules:
  0.0 79.2 jit_solution(16533977097986799367)
XLA Ops:
  0.6 72.6 %shard_map.84 = (bf16[256,16,128]{2,1,0:T(8,128)(2,1)}, bf16[256,16,128]{2,1,0:T(8,128)(2,1)}, bf16[256,8,128]{2,1,0:T(8,128)(2,1)}, bf16[256,8,128]{2,1,0:T(8,128)(2,1)}) custom-call(s32[16]{0:T(128)} %doc_ref.1, bf16[256,16,128]{2,1,0:T(8,128)(2,1)} %q_ref.1, bf16[256,16,128]{2,1,0:T(8,128)(2,1)} %g_ref.1, bf16[256,8,128]{2,1,0:T(8,128)(2,1)} %k_ref.1, ...), custom_call_target="tpu_custom_call" | custom-call | tf_op jit(solution)/shard_map/pallas_call | solution.py:268
  73.3 0.0 copy-start
  73.3 2.5 %copy.13 = bf16[256,16,128]{2,1,0:T(8,128)(2,1)} copy(bf16[256,16,128]{2,1,0:T(8,128)(2,1)} %get-tuple-element.8) | data formatting | bytes 2097152
  75.8 0.0 copy-done
  75.8 0.0 copy-start.2
  75.8 1.0 %copy.14 = bf16[256,16,128]{2,1,0:T(8,128)(2,1)} copy(bf16[256,16,128]{2,1,0:T(8,128)(2,1)S(1)} %copy-done) | data formatting | bytes 2097152
  76.7 0.4 copy-done.2
  77.2 0.0 copy-start.1
  77.2 0.8 %copy.15 = bf16[256,8,128]{2,1,0:T(8,128)(2,1)} copy(bf16[256,8,128]{2,1,0:T(8,128)(2,1)S(1)} %copy-done.2) | data formatting | bytes 1048576
  77.9 0.4 copy-done.1
  78.4 0.8 %copy.16 = bf16[256,8,128]{2,1,0:T(8,128)(2,1)} copy(bf16[256,8,128]{2,1,0:T(8,128)(2,1)S(1)} %copy-done.1) | data formatting | bytes 1048576
Async XLA Ops:
  73.3 2.5 %copy-start = (bf16[256,16,128]{2,1,0:T(8,128)(2,1)S(1)}, bf16[256,16,128]{2,1,0:T(8,128)(2,1)}, u32[]{:S(2)}) copy-start(bf16[256,16,128]{2,1,0:T(8,128)(2,1)} %get-tuple-element.9) | copy-start | bytes 3145732
  75.8 1.4 %copy-start.2 = (bf16[256,8,128]{2,1,0:T(8,128)(2,1)S(1)}, bf16[256,8,128]{2,1,0:T(8,128)(2,1)}, u32[]{:S(2)}) copy-start(bf16[256,8,128]{2,1,0:T(8,128)(2,1)} %get-tuple-element.10) | copy-start | bytes 1572868
  77.2 1.2 %copy-start.1 = (bf16[256,8,128]{2,1,0:T(8,128)(2,1)S(1)}, bf16[256,8,128]{2,1,0:T(8,128)(2,1)}, u32[]{:S(2)}) copy-start(bf16[256,8,128]{2,1,0:T(8,128)(2,1)} %get-tuple-element.11) | copy-start | bytes 1572868

commit v3 on v2

v3 whole, which is shorter than its diff:
```python
import functools

import jax
import jax.numpy as jnp
from jax import lax
from jax.experimental import pallas as pl
from jax.experimental.pallas import tpu as pltpu
from jax.sharding import PartitionSpec as P

WINDOW = 1024
SCALING = 168.0 ** (-0.5)
LOG2E = 1.4426950408889634
MASKED = -1e30
LAG = 2
MESH = pl.DeviceIdType.MESH
F32 = jnp.float32
BF16 = jnp.bfloat16


def kernel(
    size, reach, doc_ref, q_ref, g_ref, k_ref, v_ref,
    out_ref, dq_ref, dk_ref, dv_ref,
    k_own, v_own, kv_all, part, back, relay, bias,
    kv_send, kv_recv, grad_send, grad_recv, relay_recv, pass_send,
):
    groups, rows, dim = k_ref.shape
    units, lanes = q_ref.shape[1:3]
    step = rows // units
    per = lanes // step
    depth = reach * rows + step
    me = lax.axis_index("ctx")
    plane, spot = me // reach, me % reach
    planes = size // reach
    distances = range(1, reach + 1)
    near = range(1, reach)

    def slot(d):
        return pl.ds((reach - d) * rows, rows)

    def remote(src, dst, send, recv, to):
        return pltpu.make_async_remote_copy(
            src_ref=src, dst_ref=dst, send_sem=send, recv_sem=recv,
            device_id={"ctx": to}, device_id_type=MESH,
        )

    def outward(d, g):
        return remote(
            kv_all.at[g, :, slot(0)], kv_all.at[g, :, slot(d)],
            kv_send.at[d - 1, g], kv_recv.at[d - 1, g], me + d,
        )

    def passed(d, g):
        return remote(
            kv_all.at[g, :, slot(reach)], kv_all.at[g, :, slot(d)],
            pass_send.at[d - 1, g], kv_recv.at[d - 1, g], me - (reach - d),
        )

    def homeward(d, g):
        return remote(
            part.at[d - 1, g], back.at[d - 1, g],
            grad_send.at[d - 1, g], grad_recv.at[d - 1, g], me - d,
        )

    def relayed(d, g):
        return remote(
            part.at[d - 1, g], relay.at[d - 1, g],
            grad_send.at[d - 1, g], relay_recv.at[d - 1, g], me + (reach - d),
        )

    barrier = pltpu.get_barrier_semaphore()

    def greet(to):
        pl.semaphore_signal(barrier, inc=1, device_id={"ctx": to}, device_id_type=MESH)

    for o in near:
        greet(plane * reach + (spot + o) % reach)

    @pl.when(plane > 0)
    def _():
        greet(me - reach)

    @pl.when(plane < planes - 1)
    def _():
        greet(me + reach)

    peers = (reach - 1) + jnp.minimum(plane, 1) + jnp.minimum(planes - 1 - plane, 1)
    pl.semaphore_wait(barrier, peers)

    @pl.loop(0, groups)
    def _(g):
        kv_all[g, 0, slot(0), :] = k_ref[g]
        kv_all[g, 1, slot(0), :] = v_ref[g]

        @pl.when(plane < planes - 1)
        def _():
            outward(reach, g).start()

        for d in near:
            @pl.when(spot + d < reach)
            def _():
                outward(d, g).start()

    column = lax.broadcasted_iota(jnp.int32, (1, step), 1)
    at = lax.broadcasted_iota(jnp.int32, (depth, step), 0)
    for u in range(units):
        position = me * rows + u * step + column
        first = jnp.maximum(position - (WINDOW - 1), 0)
        end = jnp.int32(0)
        for n in range(doc_ref.shape[0]):
            end = end + doc_ref[n]
            first = jnp.maximum(first, jnp.where(position >= end, end, 0))
        first = first - (me - reach) * rows - u * step
        seen = (at >= first) & (at <= column + reach * rows)
        mask = jnp.where(seen, 0.0, MASKED).astype(F32)
        for n in range(per):
            bias[u, :, n * step:(n + 1) * step] = mask

    for d in distances:
        @pl.when(me < d)
        def _():
            kv_all[:, :, slot(d), :] = jnp.zeros((groups, 2, rows, dim), BF16)

    def across(left, right):
        return lax.dot_general(left, right, (((1,), (1,)), ((), ())), preferred_element_type=F32)

    def product(left, right):
        return jnp.dot(left, right, preferred_element_type=F32)

    def flipped(array):
        return array.astype(F32).T.astype(BF16)

    def send_far(g):
        @pl.when(plane > 0)
        def _():
            for d in near:
                @pl.when(spot >= reach - d)
                def _():
                    remote(
                        part.at[d - 1, g], relay.at[d - 1, g],
                        grad_send.at[d - 1, g], relay_recv.at[d - 1, g], me - (reach - d),
                    ).wait_recv()
                    total = part[reach - 1, g].astype(F32) + relay[d - 1, g].astype(F32)
                    part[reach - 1, g] = total.astype(BF16)
            homeward(reach, g).start()

    @pl.loop(0, groups)
    def _(g):
        @pl.when(plane > 0)
        def _():
            outward(reach, g).wait_recv()
            for d in near:
                @pl.when(spot >= reach - d)
                def _():
                    passed(d, g).start()

        for d in near:
            @pl.when(me >= d)
            def _():
                outward(d, g).wait_recv()

        each = range(units)
        reached = [pl.ds(u * step, depth) for u in each]
        query = [q_ref[g, u] for u in each]
        grad = [g_ref[g, u] for u in each]
        products = [across(kv_all[g, 0, reached[u], :], query[u]) for u in each]
        weight_grad = [across(kv_all[g, 1, reached[u], :], grad[u]) for u in each]
        key_turned, value_turned = flipped(kv_all[g, 0]), flipped(kv_all[g, 1])
        key_grad, value_grad = [], []
        for u in each:
            scores = products[u] * (SCALING * LOG2E) + bias[u]
            expo = jnp.exp2(scores - jnp.max(scores, axis=0, keepdims=True))
            inverse = 1.0 / jnp.sum(expo, axis=0, keepdims=True)
            row_total = jnp.sum(expo * weight_grad[u], axis=0, keepdims=True) * inverse
            weights = expo * inverse
            rounded = weights.astype(BF16)
            score_grad = (weights * (weight_grad[u] - row_total)).astype(BF16)
            key_grad.append(product(score_grad, query[u]) * SCALING)
            value_grad.append(product(rounded, grad[u]))
            low = u * step
            out_ref[g, u] = product(value_turned[:, low:low + depth], rounded).T.astype(BF16)
            turned = product(key_turned[:, low:low + depth], score_grad) * SCALING
            dq_ref[g, u] = turned.T.astype(BF16)

        def total(shares, low):
            found = [
                share[low - u * step:low - u * step + step]
                for u, share in enumerate(shares)
                if 0 <= low - u * step < depth
            ]
            return functools.reduce(jnp.add, found)

        for n in range(units):
            inner = slice(n * step, (n + 1) * step)
            k_own[g, inner] = total(key_grad, reach * rows + n * step)
            v_own[g, inner] = total(value_grad, reach * rows + n * step)
            for d in distances:
                low = (reach - d) * rows + n * step
                part[d - 1, g, 0, inner] = total(key_grad, low).astype(BF16)
                part[d - 1, g, 1, inner] = total(value_grad, low).astype(BF16)
        for d in near:
            @pl.when(spot >= d)
            def _():
                homeward(d, g).start()

            @pl.when((spot < d) & (plane > 0))
            def _():
                relayed(d, g).start()

        @pl.when(g >= LAG)
        def _():
            send_far(g - LAG)

    @pl.loop(groups - LAG, groups)
    def _(g):
        send_far(g)

    def add_back(d, g):
        homeward(d, g).wait_recv()
        k_own[g] += back[d - 1, g, 0].astype(F32)
        v_own[g] += back[d - 1, g, 1].astype(F32)

    @pl.loop(0, groups)
    def _(g):
        for d in near:
            @pl.when(spot + d < reach)
            def _():
                add_back(d, g)

        @pl.when(plane < planes - 1)
        def _():
            add_back(reach, g)

        dk_ref[g] = k_own[g].astype(BF16)
        dv_ref[g] = v_own[g].astype(BF16)

    @pl.loop(0, groups)
    def _(g):
        @pl.when(plane < planes - 1)
        def _():
            outward(reach, g).wait_send()

        @pl.when(plane > 0)
        def _():
            homeward(reach, g).wait_send()

        for d in near:
            @pl.when(spot + d < reach)
            def _():
                outward(d, g).wait_send()

            @pl.when((plane > 0) & (spot >= reach - d))
            def _():
                passed(d, g).wait_send()

            @pl.when(me >= d)
            def _():
                homeward(d, g).wait_send()


def body(queries, keys, values, out_grad, doc_lengths):
    rows, heads, dim = queries.shape
    groups = keys.shape[1]
    per = heads // groups
    step = 128
    units = rows // step
    size = lax.axis_size("ctx")
    reach = min(WINDOW, rows * size // 4) // rows
    span = (reach + 1) * rows

    def split(array):
        array = array.reshape(units, step, groups, per, dim).transpose(2, 0, 3, 1, 4)
        return array.reshape(groups, units, per * step, dim)

    def joined(array):
        array = array.reshape(groups, units, per, step, dim).transpose(1, 3, 0, 2, 4)
        return array.reshape(rows, heads, dim)

    vmem = pl.BlockSpec(memory_space=pltpu.VMEM)
    dma = pltpu.SemaphoreType.DMA((reach, groups))
    wide = jax.ShapeDtypeStruct((groups, units, per * step, dim), BF16)
    narrow = jax.ShapeDtypeStruct((groups, rows, dim), BF16)
    shares = pltpu.VMEM((reach, groups, 2, rows, dim), BF16)
    out, dq, dk, dv = pl.pallas_call(
        functools.partial(kernel, size, reach),
        out_shape=(wide, wide, narrow, narrow),
        in_specs=[pl.BlockSpec(memory_space=pltpu.SMEM)] + [vmem] * 4,
        out_specs=(vmem,) * 4,
        scratch_shapes=[
            pltpu.VMEM((groups, rows, dim), F32),
            pltpu.VMEM((groups, rows, dim), F32),
            pltpu.VMEM((groups, 2, span, dim), BF16),
            shares, shares, shares,
            pltpu.VMEM((units, reach * rows + step, per * step), F32),
            dma, dma, dma, dma, dma, dma,
        ],
        compiler_params=pltpu.CompilerParams(
            collective_id=0, has_side_effects=True, vmem_limit_bytes=48 * 2**20
        ),
    )(doc_lengths, split(queries), split(out_grad), keys.transpose(1, 0, 2), values.transpose(1, 0, 2))
    return joined(out), joined(dq), dk.transpose(1, 0, 2), dv.transpose(1, 0, 2)


def solution(mesh):
    spec = P(("dp", "ctx"), "head", None)
    return jax.shard_map(
        body,
        mesh=mesh,
        in_specs=(spec, spec, spec, spec, P("dp")),
        out_specs=(spec, spec, spec, spec),
        check_vma=False,
    )
```

time: 79.4 us -> 80.2 us (1.010)
  local copies, waits for them, and re-layouts: 5.88 us -> 10.1 us
  Pallas kernels: 72.6 us -> 69.2 us
    transpose x0 -> x3, local copies, waits for them, and re-layouts: none -> 4.28 us  [the longest x2 4.1 us: joined(): array.reshape(groups, units, per, step, dim).transpose(1, 3, 0, 2, 4)]
    pallas_call x1, Pallas kernels: 72.6 us -> 69.2 us  [body(): pl.pallas_call(functools.partial(kernel, size, reach), out_shape=(wide, w...]
    unnamed x10, local copies, waits for them, and re-layouts: 5.88 us -> 2.94 us
    reshape x0 -> x2, local copies, waits for them, and re-layouts: none -> 2.84 us  [split(): array.reshape(units, step, groups, per, dim).transpose(2, 0, 3, 1, 4)]
where the time goes in v3:
time: 80.2 us; the launch traced here: 80 us
  Pallas kernels  69.2 us (86%)
  local copies, waits for them, and re-layouts  10.1 us (13%)
    pallas_call x1, Pallas kernels, body(): pl.pallas_call(functools.partial(kernel, size, reach), out_shape=(wide, w...  69.2 us
    transpose x2, local copies, waits for them, and re-layouts, joined(): array.reshape(groups, units, per, step, dim).transpose(1, 3, 0, 2, 4)  4.1 us
    unnamed x10, local copies, waits for them, and re-layouts  2.94 us
    reshape x2, local copies, waits for them, and re-layouts, split(): array.reshape(units, step, groups, per, dim).transpose(2, 0, 3, 1, 4)  2.84 us

profile of v3, /device:TPU:0, one launch (start us, length us, event | category | flops | bytes accessed | tf_op | source)
XLA Modules:
  0.0 80.0 jit_solution(3373628067636490989)
XLA Ops:
  0.6 0.0 copy-start.1
  0.6 1.6 %copy.9 = bf16[2,128,8,2,128]{4,1,3,0,2:T(8,128)(2,1)S(1)} copy(bf16[2,128,8,2,128]{4,3,2,1,0:T(2,128)(2,1)} %bitcast.28) | data formatting | bytes 2097152 | tf_op jit(solution)/shard_map/reshape | solution.py:271
  2.2 0.0 copy-done.1
  2.2 0.0 copy-start.2
  2.2 0.0 copy-start.3
  2.3 1.3 %copy.10 = bf16[2,128,8,2,128]{4,1,3,0,2:T(8,128)(2,1)} copy(bf16[2,128,8,2,128]{4,3,2,1,0:T(2,128)(2,1)S(1)} %bitcast.29) | data formatting | bytes 2097152 | tf_op jit(solution)/shard_map/reshape | solution.py:271
  3.5 0.0 copy-done.2
  3.5 0.0 copy-done.3
  3.5 0.2 copy_bitcast_fusion
  3.7 0.0 copy-start
  3.7 0.6 copy-done
  4.4 69.2 %shard_map.84 = (bf16[8,2,256,128]{3,2,1,0:T(8,128)(2,1)S(1)}, bf16[8,2,256,128]{3,2,1,0:T(8,128)(2,1)S(1)}, bf16[8,256,128]{2,1,0:T(8,128)(2,1)S(1)}, bf16[8,256,128]{2,1,0:T(8,128)(2,1)S(1)}) custom-call(s32[16]{0:T(128)S(1)} %copy-done, bf16[8,2,256,128]{3,2,1,0:T(8,128)(2,1)S(1)} %bitcast.22, bf16[8,2,256,128]{3,2,1,0:T(8,128)(2,1)} %bitcast.27, ...), custom_call_target="tpu_custom_call" | custom-call | tf_op jit(solution)/shard_map/pallas_call | solution.py:283
  73.6 2.0 %copy.13 = bf16[2,128,8,2,128]{4,3,2,1,0:T(2,128)(2,1)} copy(bf16[2,128,8,2,128]{4,1,3,0,2:T(8,128)(2,1)S(1)} %bitcast.24) | data formatting | bytes 2097152 | tf_op jit(solution)/shard_map/transpose | solution.py:275
  75.7 2.0 %copy.14 = bf16[2,128,8,2,128]{4,3,2,1,0:T(2,128)(2,1)} copy(bf16[2,128,8,2,128]{4,1,3,0,2:T(8,128)(2,1)S(1)} %bitcast.23) | data formatting | bytes 2097152 | tf_op jit(solution)/shard_map/transpose | solution.py:275
  77.7 1.1 %copy.15 = bf16[256,8,128]{2,1,0:T(8,128)(2,1)} copy(bf16[256,8,128]{2,0,1:T(8,128)(2,1)S(1)} %bitcast.26) | data formatting | bytes 1048576
  78.9 1.1 %copy.16 = bf16[256,8,128]{2,1,0:T(8,128)(2,1)} copy(bf16[256,8,128]{2,0,1:T(8,128)(2,1)S(1)} %bitcast.25) | data formatting | bytes 1048576
Async XLA Ops:
  0.6 1.6 %copy-start.1 = (bf16[256,16,128]{2,1,0:T(8,128)(2,1)S(1)}, bf16[256,16,128]{2,1,0:T(8,128)(2,1)}, u32[]{:S(2)}) copy-start(bf16[256,16,128]{2,1,0:T(8,128)(2,1)} %param.8) | copy-start | bytes 3145732
  2.2 1.3 %copy-start.2 = (bf16[256,8,128]{2,1,0:T(8,128)(2,1)S(1)}, bf16[256,8,128]{2,1,0:T(8,128)(2,1)}, u32[]{:S(2)}) copy-start(bf16[256,8,128]{2,1,0:T(8,128)(2,1)} %param.7) | copy-start | bytes 1572868
  2.2 1.3 %copy-start.3 = (bf16[256,8,128]{2,1,0:T(8,128)(2,1)S(1)}, bf16[256,8,128]{2,1,0:T(8,128)(2,1)}, u32[]{:S(2)}) copy-start(bf16[256,8,128]{2,1,0:T(8,128)(2,1)} %param.6) | copy-start | bytes 1572868
  3.7 0.7 copy-start

commit v4 on v3

--- a/solution.py
+++ b/solution.py
@@ -11,7 +11,6 @@
 SCALING = 168.0 ** (-0.5)
 LOG2E = 1.4426950408889634
 MASKED = -1e30
-LAG = 2
 MESH = pl.DeviceIdType.MESH
 F32 = jnp.float32
 BF16 = jnp.bfloat16
@@ -20,8 +19,8 @@
 def kernel(
     size, reach, doc_ref, q_ref, g_ref, k_ref, v_ref,
     out_ref, dq_ref, dk_ref, dv_ref,
-    k_own, v_own, kv_all, part, back, relay, bias,
-    kv_send, kv_recv, grad_send, grad_recv, relay_recv, pass_send,
+    k_own, v_own, kv_all, part, back, bias,
+    kv_send, kv_recv, grad_send, grad_recv,
 ):
     groups, rows, dim = k_ref.shape
     units, lanes = q_ref.shape[1:3]
@@ -29,10 +28,7 @@
     per = lanes // step
     depth = reach * rows + step
     me = lax.axis_index("ctx")
-    plane, spot = me // reach, me % reach
-    planes = size // reach
     distances = range(1, reach + 1)
-    near = range(1, reach)
 
     def slot(d):
         return pl.ds((reach - d) * rows, rows)
@@ -49,41 +45,24 @@
             kv_send.at[d - 1, g], kv_recv.at[d - 1, g], me + d,
         )
 
-    def passed(d, g):
-        return remote(
-            kv_all.at[g, :, slot(reach)], kv_all.at[g, :, slot(d)],
-            pass_send.at[d - 1, g], kv_recv.at[d - 1, g], me - (reach - d),
-        )
-
     def homeward(d, g):
         return remote(
             part.at[d - 1, g], back.at[d - 1, g],
             grad_send.at[d - 1, g], grad_recv.at[d - 1, g], me - d,
         )
 
-    def relayed(d, g):
-        return remote(
-            part.at[d - 1, g], relay.at[d - 1, g],
-            grad_send.at[d - 1, g], relay_recv.at[d - 1, g], me + (reach - d),
-        )
-
     barrier = pltpu.get_barrier_semaphore()
 
-    def greet(to):
-        pl.semaphore_signal(barrier, inc=1, device_id={"ctx": to}, device_id_type=MESH)
-
-    for o in near:
-        greet(plane * reach + (spot + o) % reach)
-
-    @pl.when(plane > 0)
-    def _():
-        greet(me - reach)
-
-    @pl.when(plane < planes - 1)
-    def _():
-        greet(me + reach)
-
-    peers = (reach - 1) + jnp.minimum(plane, 1) + jnp.minimum(planes - 1 - plane, 1)
+    for d in distances:
+        @pl.when(me + d < size)
+        def _():
+            pl.semaphore_signal(barrier, inc=1, device_id={"ctx": me + d}, device_id_type=MESH)
+
+        @pl.when(me >= d)
+        def _():
+            pl.semaphore_signal(barrier, inc=1, device_id={"ctx": me - d}, device_id_type=MESH)
+
+    peers = jnp.minimum(me, reach) + jnp.minimum(size - 1 - me, reach)
     pl.semaphore_wait(barrier, peers)
 
     @pl.loop(0, groups)
@@ -91,12 +70,8 @@
         kv_all[g, 0, slot(0), :] = k_ref[g]
         kv_all[g, 1, slot(0), :] = v_ref[g]
 
-        @pl.when(plane < planes - 1)
-        def _():
-            outward(reach, g).start()
-
-        for d in near:
-            @pl.when(spot + d < reach)
+        for d in distances:
+            @pl.when(me + d < size)
             def _():
                 outward(d, g).start()
 
@@ -129,31 +104,9 @@
     def flipped(array):
         return array.astype(F32).T.astype(BF16)
 
-    def send_far(g):
-        @pl.when(plane > 0)
-        def _():
-            for d in near:
-                @pl.when(spot >= reach - d)
-                def _():
-                    remote(
-                        part.at[d - 1, g], relay.at[d - 1, g],
-                        grad_send.at[d - 1, g], relay_recv.at[d - 1, g], me - (reach - d),
-                    ).wait_recv()
-                    total = part[reach - 1, g].astype(F32) + relay[d - 1, g].astype(F32)
-                    part[reach - 1, g] = total.astype(BF16)
-            homeward(reach, g).start()
-
-    @pl.loop(0, groups)
-    def _(g):
-        @pl.when(plane > 0)
-        def _():
-            outward(reach, g).wait_recv()
-            for d in near:
-                @pl.when(spot >= reach - d)
-                def _():
-                    passed(d, g).start()
-
-        for d in near:
+    @pl.loop(0, groups)
+    def _(g):
+        for d in distances:
             @pl.when(me >= d)
             def _():
                 outward(d, g).wait_recv()
@@ -197,22 +150,10 @@
                 low = (reach - d) * rows + n * step
                 part[d - 1, g, 0, inner] = total(key_grad, low).astype(BF16)
                 part[d - 1, g, 1, inner] = total(value_grad, low).astype(BF16)
-        for d in near:
-            @pl.when(spot >= d)
+        for d in distances:
+            @pl.when(me >= d)
             def _():
                 homeward(d, g).start()
-
-            @pl.when((spot < d) & (plane > 0))
-            def _():
-                relayed(d, g).start()
-
-        @pl.when(g >= LAG)
-        def _():
-            send_far(g - LAG)
-
-    @pl.loop(groups - LAG, groups)
-    def _(g):
-        send_far(g)
 
     def add_back(d, g):
         homeward(d, g).wait_recv()
@@ -221,36 +162,20 @@
 
     @pl.loop(0, groups)
     def _(g):
-        for d in near:
-            @pl.when(spot + d < reach)
+        for d in distances:
+            @pl.when(me + d < size)
             def _():
                 add_back(d, g)
-
-        @pl.when(plane < planes - 1)
-        def _():
-            add_back(reach, g)
 
         dk_ref[g] = k_own[g].astype(BF16)
         dv_ref[g] = v_own[g].astype(BF16)
 
     @pl.loop(0, groups)
     def _(g):
-        @pl.when(plane < planes - 1)
-        def _():
-            outward(reach, g).wait_send()
-
-        @pl.when(plane > 0)
-        def _():
-            homeward(reach, g).wait_send()
-
-        for d in near:
-            @pl.when(spot + d < reach)
+        for d in distances:
+            @pl.when(me + d < size)
             def _():
                 outward(d, g).wait_send()
-
-            @pl.when((plane > 0) & (spot >= reach - d))
-            def _():
-                passed(d, g).wait_send()
 
             @pl.when(me >= d)
             def _():
@@ -289,9 +214,9 @@
             pltpu.VMEM((groups, rows, dim), F32),
             pltpu.VMEM((groups, rows, dim), F32),
             pltpu.VMEM((groups, 2, span, dim), BF16),
-            shares, shares, shares,
+            shares, shares,
             pltpu.VMEM((units, reach * rows + step, per * step), F32),
-            dma, dma, dma, dma, dma, dma,
+            dma, dma, dma, dma,
         ],
         compiler_params=pltpu.CompilerParams(
             collective_id=0, has_side_effects=True, vmem_limit_bytes=48 * 2**20

time: 80.2 us -> 68.9 us (0.86)
  Pallas kernels: 69.2 us -> 58 us
    pallas_call x1, Pallas kernels: 69.2 us -> 58 us  [body(): pl.pallas_call(functools.partial(kernel, size, reach), out_shape=(wide, w...]
where the time goes in v4:
time: 68.9 us; the launch traced here: 68.7 us
  Pallas kernels  58 us (84%)
  local copies, waits for them, and re-layouts  10.1 us (15%)
  between operations  0.69 us (1%)
    pallas_call x1, Pallas kernels, body(): pl.pallas_call(functools.partial(kernel, size, reach), out_shape=(wide, w...  58 us
    transpose x2, local copies, waits for them, and re-layouts, joined(): array.reshape(groups, units, per, step, dim).transpose(1, 3, 0, 2, 4)  4.1 us
    unnamed x10, local copies, waits for them, and re-layouts  2.94 us
    reshape x2, local copies, waits for them, and re-layouts, split(): array.reshape(units, step, groups, per, dim).transpose(2, 0, 3, 1, 4)  2.84 us

profile of v4, /device:TPU:0, one launch (start us, length us, event | category | flops | bytes accessed | tf_op | source)
XLA Modules:
  0.0 68.7 jit_solution(6776406853494538434)
XLA Ops:
  0.6 0.0 copy-start.1
  0.6 1.6 %copy.9 = bf16[2,128,8,2,128]{4,1,3,0,2:T(8,128)(2,1)S(1)} copy(bf16[2,128,8,2,128]{4,3,2,1,0:T(2,128)(2,1)} %bitcast.28) | data formatting | bytes 2097152 | tf_op jit(solution)/shard_map/reshape | solution.py:196
  2.2 0.0 copy-done.1
  2.2 0.0 copy-start.2
  2.2 0.0 copy-start.3
  2.3 1.3 %copy.10 = bf16[2,128,8,2,128]{4,1,3,0,2:T(8,128)(2,1)} copy(bf16[2,128,8,2,128]{4,3,2,1,0:T(2,128)(2,1)S(1)} %bitcast.29) | data formatting | bytes 2097152 | tf_op jit(solution)/shard_map/reshape | solution.py:196
  3.5 0.0 copy-done.2
  3.5 0.0 copy-done.3
  3.5 0.2 copy_bitcast_fusion
  3.7 0.0 copy-start
  3.7 0.6 copy-done
  4.4 58.0 %shard_map.84 = (bf16[8,2,256,128]{3,2,1,0:T(8,128)(2,1)S(1)}, bf16[8,2,256,128]{3,2,1,0:T(8,128)(2,1)S(1)}, bf16[8,256,128]{2,1,0:T(8,128)(2,1)S(1)}, bf16[8,256,128]{2,1,0:T(8,128)(2,1)S(1)}) custom-call(s32[16]{0:T(128)S(1)} %copy-done, bf16[8,2,256,128]{3,2,1,0:T(8,128)(2,1)S(1)} %bitcast.22, bf16[8,2,256,128]{3,2,1,0:T(8,128)(2,1)} %bitcast.27, ...), custom_call_target="tpu_custom_call" | custom-call | tf_op jit(solution)/shard_map/pallas_call | solution.py:208
  62.3 2.0 %copy.13 = bf16[2,128,8,2,128]{4,3,2,1,0:T(2,128)(2,1)} copy(bf16[2,128,8,2,128]{4,1,3,0,2:T(8,128)(2,1)S(1)} %bitcast.24) | data formatting | bytes 2097152 | tf_op jit(solution)/shard_map/transpose | solution.py:200
  64.4 2.0 %copy.14 = bf16[2,128,8,2,128]{4,3,2,1,0:T(2,128)(2,1)} copy(bf16[2,128,8,2,128]{4,1,3,0,2:T(8,128)(2,1)S(1)} %bitcast.23) | data formatting | bytes 2097152 | tf_op jit(solution)/shard_map/transpose | solution.py:200
  66.4 1.1 %copy.15 = bf16[256,8,128]{2,1,0:T(8,128)(2,1)} copy(bf16[256,8,128]{2,0,1:T(8,128)(2,1)S(1)} %bitcast.26) | data formatting | bytes 1048576
  67.6 1.1 %copy.16 = bf16[256,8,128]{2,1,0:T(8,128)(2,1)} copy(bf16[256,8,128]{2,0,1:T(8,128)(2,1)S(1)} %bitcast.25) | data formatting | bytes 1048576
Async XLA Ops:
  0.6 1.6 %copy-start.1 = (bf16[256,16,128]{2,1,0:T(8,128)(2,1)S(1)}, bf16[256,16,128]{2,1,0:T(8,128)(2,1)}, u32[]{:S(2)}) copy-start(bf16[256,16,128]{2,1,0:T(8,128)(2,1)} %param.8) | copy-start | bytes 3145732
  2.2 1.3 %copy-start.2 = (bf16[256,8,128]{2,1,0:T(8,128)(2,1)S(1)}, bf16[256,8,128]{2,1,0:T(8,128)(2,1)}, u32[]{:S(2)}) copy-start(bf16[256,8,128]{2,1,0:T(8,128)(2,1)} %param.7) | copy-start | bytes 1572868
  2.2 1.3 %copy-start.3 = (bf16[256,8,128]{2,1,0:T(8,128)(2,1)S(1)}, bf16[256,8,128]{2,1,0:T(8,128)(2,1)}, u32[]{:S(2)}) copy-start(bf16[256,8,128]{2,1,0:T(8,128)(2,1)} %param.6) | copy-start | bytes 1572868
  3.7 0.7 copy-start

commit v5 on v4

--- a/solution.py
+++ b/solution.py
@@ -11,6 +11,7 @@
 SCALING = 168.0 ** (-0.5)
 LOG2E = 1.4426950408889634
 MASKED = -1e30
+LAG = 4
 MESH = pl.DeviceIdType.MESH
 F32 = jnp.float32
 BF16 = jnp.bfloat16
@@ -19,13 +20,14 @@
 def kernel(
     size, reach, doc_ref, q_ref, g_ref, k_ref, v_ref,
     out_ref, dq_ref, dk_ref, dv_ref,
-    k_own, v_own, kv_all, part, back, bias,
+    q_wide, g_wide, k_own, v_own, kv_all, part, back, bias,
     kv_send, kv_recv, grad_send, grad_recv,
 ):
     groups, rows, dim = k_ref.shape
-    units, lanes = q_ref.shape[1:3]
-    step = rows // units
-    per = lanes // step
+    heads = q_ref.shape[1]
+    per = heads // groups
+    units, lanes = out_ref.shape[1:3]
+    step = lanes // per
     depth = reach * rows + step
     me = lax.axis_index("ctx")
     distances = range(1, reach + 1)
@@ -74,6 +76,9 @@
             @pl.when(me + d < size)
             def _():
                 outward(d, g).start()
+
+    q_wide[...] = q_ref[...].astype(F32).reshape(rows * heads, dim)
+    g_wide[...] = g_ref[...].astype(F32).reshape(rows * heads, dim)
 
     column = lax.broadcasted_iota(jnp.int32, (1, step), 1)
     at = lax.broadcasted_iota(jnp.int32, (depth, step), 0)
@@ -104,6 +109,23 @@
     def flipped(array):
         return array.astype(F32).T.astype(BF16)
 
+    def head_rows(wide, g, u):
+        starts = [u * step * heads + g * per + n for n in range(per)]
+        return jnp.concatenate(
+            [wide[pl.ds(start, step, stride=heads), :] for start in starts], 0
+        ).astype(BF16)
+
+    def finish(g):
+        for d in distances:
+            @pl.when(me + d < size)
+            def _():
+                homeward(d, g).wait_recv()
+                k_own[g] += back[d - 1, g, 0].astype(F32)
+                v_own[g] += back[d - 1, g, 1].astype(F32)
+
+        dk_ref[g] = k_own[g].astype(BF16)
+        dv_ref[g] = v_own[g].astype(BF16)
+
     @pl.loop(0, groups)
     def _(g):
         for d in distances:
@@ -113,8 +135,8 @@
 
         each = range(units)
         reached = [pl.ds(u * step, depth) for u in each]
-        query = [q_ref[g, u] for u in each]
-        grad = [g_ref[g, u] for u in each]
+        query = [head_rows(q_wide, g, u) for u in each]
+        grad = [head_rows(g_wide, g, u) for u in each]
         products = [across(kv_all[g, 0, reached[u], :], query[u]) for u in each]
         weight_grad = [across(kv_all[g, 1, reached[u], :], grad[u]) for u in each]
         key_turned, value_turned = flipped(kv_all[g, 0]), flipped(kv_all[g, 1])
@@ -155,20 +177,13 @@
             def _():
                 homeward(d, g).start()
 
-    def add_back(d, g):
-        homeward(d, g).wait_recv()
-        k_own[g] += back[d - 1, g, 0].astype(F32)
-        v_own[g] += back[d - 1, g, 1].astype(F32)
-
-    @pl.loop(0, groups)
-    def _(g):
-        for d in distances:
-            @pl.when(me + d < size)
-            def _():
-                add_back(d, g)
-
-        dk_ref[g] = k_own[g].astype(BF16)
-        dv_ref[g] = v_own[g].astype(BF16)
+        @pl.when(g >= LAG)
+        def _():
+            finish(g - LAG)
+
+    @pl.loop(groups - LAG, groups)
+    def _(g):
+        finish(g)
 
     @pl.loop(0, groups)
     def _(g):
@@ -191,10 +206,6 @@
     size = lax.axis_size("ctx")
     reach = min(WINDOW, rows * size // 4) // rows
     span = (reach + 1) * rows
-
-    def split(array):
-        array = array.reshape(units, step, groups, per, dim).transpose(2, 0, 3, 1, 4)
-        return array.reshape(groups, units, per * step, dim)
 
     def joined(array):
         array = array.reshape(groups, units, per, step, dim).transpose(1, 3, 0, 2, 4)
@@ -211,6 +222,8 @@
         in_specs=[pl.BlockSpec(memory_space=pltpu.SMEM)] + [vmem] * 4,
         out_specs=(vmem,) * 4,
         scratch_shapes=[
+            pltpu.VMEM((rows * heads, dim), F32),
+            pltpu.VMEM((rows * heads, dim), F32),
             pltpu.VMEM((groups, rows, dim), F32),
             pltpu.VMEM((groups, rows, dim), F32),
             pltpu.VMEM((groups, 2, span, dim), BF16),
@@ -221,7 +234,7 @@
         compiler_params=pltpu.CompilerParams(
             collective_id=0, has_side_effects=True, vmem_limit_bytes=48 * 2**20
         ),
-    )(doc_lengths, split(queries), split(out_grad), keys.transpose(1, 0, 2), values.transpose(1, 0, 2))
+    )(doc_lengths, queries, out_grad, keys.transpose(1, 0, 2), values.transpose(1, 0, 2))
     return joined(out), joined(dq), dk.transpose(1, 0, 2), dv.transpose(1, 0, 2)
 
 

time: 68.9 us -> 67.4 us (0.978)
  local copies, waits for them, and re-layouts: 10.1 us -> 8.5 us
    reshape x2 -> x0, local copies, waits for them, and re-layouts: 2.84 us -> none  [split(): array.reshape(units, step, groups, per, dim).transpose(2, 0, 3, 1, 4)]
    transpose x1, local copies, waits for them, and re-layouts: 0.19 us -> 1.48 us  [body(): values.transpose(1, 0, 2)]
    unnamed x10 -> x6, local copies, waits for them, and re-layouts: 2.94 us -> 2.93 us
where the time goes in v5:
time: 67.4 us; the launch traced here: 67.2 us
  Pallas kernels  58 us (86%)
  local copies, waits for them, and re-layouts  8.5 us (13%)
    pallas_call x1, Pallas kernels, body(): pl.pallas_call(functools.partial(kernel, size, reach), out_shape=(wide, w...  58 us
    transpose x2, local copies, waits for them, and re-layouts, joined(): array.reshape(groups, units, per, step, dim).transpose(1, 3, 0, 2, 4)  4.1 us
    unnamed x6, local copies, waits for them, and re-layouts  2.93 us
    transpose x1, local copies, waits for them, and re-layouts, body(): values.transpose(1, 0, 2)  1.48 us

profile of v5, /device:TPU:0, one launch (start us, length us, event | category | flops | bytes accessed | tf_op | source)
XLA Modules:
  0.0 67.2 jit_solution(15059609152856754792)
XLA Ops:
  0.6 0.0 copy-start
  0.6 1.5 %copy_bitcast_fusion = (bf16[8,256,128]{2,1,0:T(8,128)(2,1)S(1)}, bf16[8,256,128]{2,1,0:T(8,128)(2,1)S(1)}) fusion(bf16[256,8,128]{2,1,0:T(8,128)(2,1)} %param.7, bf16[256,8,128]{2,1,0:T(8,128)(2,1)} %param.6), kind=kLoop, calls=%fused_computation | loop fusion | bytes 2097152 | tf_op jit(solution)/shard_map/transpose | solution.py:237
  2.1 0.0 copy-start.1
  2.1 0.0 copy-done
  2.2 0.6 copy-done.1
  2.8 58.0 %shard_map.84 = (bf16[8,2,256,128]{3,2,1,0:T(8,128)(2,1)S(1)}, bf16[8,2,256,128]{3,2,1,0:T(8,128)(2,1)S(1)}, bf16[8,256,128]{2,1,0:T(8,128)(2,1)S(1)}, bf16[8,256,128]{2,1,0:T(8,128)(2,1)S(1)}) custom-call(s32[16]{0:T(128)S(1)} %copy-done.1, bf16[256,16,128]{2,1,0:T(8,128)(2,1)S(1)} %copy-done, bf16[256,16,128]{2,1,0:T(8,128)(2,1)} %g_ref.1, ...), custom_call_target="tpu_custom_call" | custom-call | tf_op jit(solution)/shard_map/pallas_call | solution.py:219
  60.8 2.0 %copy.11 = bf16[2,128,8,2,128]{4,3,2,1,0:T(2,128)(2,1)} copy(bf16[2,128,8,2,128]{4,1,3,0,2:T(8,128)(2,1)S(1)} %bitcast.15) | data formatting | bytes 2097152 | tf_op jit(solution)/shard_map/transpose | solution.py:211
  62.8 2.0 %copy.12 = bf16[2,128,8,2,128]{4,3,2,1,0:T(2,128)(2,1)} copy(bf16[2,128,8,2,128]{4,1,3,0,2:T(8,128)(2,1)S(1)} %bitcast.14) | data formatting | bytes 2097152 | tf_op jit(solution)/shard_map/transpose | solution.py:211
  64.9 1.1 %copy.13 = bf16[256,8,128]{2,1,0:T(8,128)(2,1)} copy(bf16[256,8,128]{2,0,1:T(8,128)(2,1)S(1)} %bitcast.17) | data formatting | bytes 1048576
  66.0 1.1 %copy.14 = bf16[256,8,128]{2,1,0:T(8,128)(2,1)} copy(bf16[256,8,128]{2,0,1:T(8,128)(2,1)S(1)} %bitcast.16) | data formatting | bytes 1048576
Async XLA Ops:
  0.6 1.5 %copy-start = (bf16[256,16,128]{2,1,0:T(8,128)(2,1)S(1)}, bf16[256,16,128]{2,1,0:T(8,128)(2,1)}, u32[]{:S(2)}) copy-start(bf16[256,16,128]{2,1,0:T(8,128)(2,1)} %q_ref.1) | copy-start | bytes 3145732
  2.1 0.7 copy-start.1

commit v6 on v5

--- a/solution.py
+++ b/solution.py
@@ -20,14 +20,14 @@
 def kernel(
     size, reach, doc_ref, q_ref, g_ref, k_ref, v_ref,
     out_ref, dq_ref, dk_ref, dv_ref,
-    q_wide, g_wide, k_own, v_own, kv_all, part, back, bias,
+    q_wide, g_wide, k_wide, v_wide, out_wide, dq_wide, k_own, v_own, kv_all, part, back, bias,
     kv_send, kv_recv, grad_send, grad_recv,
 ):
-    groups, rows, dim = k_ref.shape
+    rows, groups, dim = k_ref.shape
     heads = q_ref.shape[1]
     per = heads // groups
-    units, lanes = out_ref.shape[1:3]
-    step = lanes // per
+    step = 128
+    units = rows // step
     depth = reach * rows + step
     me = lax.axis_index("ctx")
     distances = range(1, reach + 1)
@@ -64,13 +64,15 @@
         def _():
             pl.semaphore_signal(barrier, inc=1, device_id={"ctx": me - d}, device_id_type=MESH)
 
+    k_wide[...] = k_ref[...].astype(F32).reshape(rows * groups, dim)
+    v_wide[...] = v_ref[...].astype(F32).reshape(rows * groups, dim)
     peers = jnp.minimum(me, reach) + jnp.minimum(size - 1 - me, reach)
     pl.semaphore_wait(barrier, peers)
 
     @pl.loop(0, groups)
     def _(g):
-        kv_all[g, 0, slot(0), :] = k_ref[g]
-        kv_all[g, 1, slot(0), :] = v_ref[g]
+        kv_all[g, 0, slot(0), :] = k_wide[pl.ds(g, rows, stride=groups), :].astype(BF16)
+        kv_all[g, 1, slot(0), :] = v_wide[pl.ds(g, rows, stride=groups), :].astype(BF16)
 
         for d in distances:
             @pl.when(me + d < size)
@@ -114,6 +116,11 @@
         return jnp.concatenate(
             [wide[pl.ds(start, step, stride=heads), :] for start in starts], 0
         ).astype(BF16)
+
+    def store_heads(wide, g, u, array):
+        for n in range(per):
+            start = u * step * heads + g * per + n
+            wide[pl.ds(start, step, stride=heads), :] = array[n * step:(n + 1) * step]
 
     def finish(g):
         for d in distances:
@@ -152,9 +159,9 @@
             key_grad.append(product(score_grad, query[u]) * SCALING)
             value_grad.append(product(rounded, grad[u]))
             low = u * step
-            out_ref[g, u] = product(value_turned[:, low:low + depth], rounded).T.astype(BF16)
+            store_heads(out_wide, g, u, product(value_turned[:, low:low + depth], rounded).T)
             turned = product(key_turned[:, low:low + depth], score_grad) * SCALING
-            dq_ref[g, u] = turned.T.astype(BF16)
+            store_heads(dq_wide, g, u, turned.T)
 
         def total(shares, low):
             found = [
@@ -181,6 +188,9 @@
         def _():
             finish(g - LAG)
 
+    out_ref[...] = out_wide[...].reshape(rows, heads, dim).astype(BF16)
+    dq_ref[...] = dq_wide[...].reshape(rows, heads, dim).astype(BF16)
+
     @pl.loop(groups - LAG, groups)
     def _(g):
         finish(g)
@@ -202,18 +212,13 @@
     groups = keys.shape[1]
     per = heads // groups
     step = 128
-    units = rows // step
     size = lax.axis_size("ctx")
     reach = min(WINDOW, rows * size // 4) // rows
     span = (reach + 1) * rows
 
-    def joined(array):
-        array = array.reshape(groups, units, per, step, dim).transpose(1, 3, 0, 2, 4)
-        return array.reshape(rows, heads, dim)
-
     vmem = pl.BlockSpec(memory_space=pltpu.VMEM)
     dma = pltpu.SemaphoreType.DMA((reach, groups))
-    wide = jax.ShapeDtypeStruct((groups, units, per * step, dim), BF16)
+    wide = jax.ShapeDtypeStruct(queries.shape, BF16)
     narrow = jax.ShapeDtypeStruct((groups, rows, dim), BF16)
     shares = pltpu.VMEM((reach, groups, 2, rows, dim), BF16)
     out, dq, dk, dv = pl.pallas_call(
@@ -224,18 +229,22 @@
         scratch_shapes=[
             pltpu.VMEM((rows * heads, dim), F32),
             pltpu.VMEM((rows * heads, dim), F32),
+            pltpu.VMEM((rows * groups, dim), F32),
+            pltpu.VMEM((rows * groups, dim), F32),
+            pltpu.VMEM((rows * heads, dim), F32),
+            pltpu.VMEM((rows * heads, dim), F32),
             pltpu.VMEM((groups, rows, dim), F32),
             pltpu.VMEM((groups, rows, dim), F32),
             pltpu.VMEM((groups, 2, span, dim), BF16),
             shares, shares,
-            pltpu.VMEM((units, reach * rows + step, per * step), F32),
+            pltpu.VMEM((rows // step, reach * rows + step, per * step), F32),
             dma, dma, dma, dma,
         ],
         compiler_params=pltpu.CompilerParams(
             collective_id=0, has_side_effects=True, vmem_limit_bytes=48 * 2**20
         ),
-    )(doc_lengths, queries, out_grad, keys.transpose(1, 0, 2), values.transpose(1, 0, 2))
-    return joined(out), joined(dq), dk.transpose(1, 0, 2), dv.transpose(1, 0, 2)
+    )(doc_lengths, queries, out_grad, keys, values)
+    return out, dq, dk.transpose(1, 0, 2), dv.transpose(1, 0, 2)
 
 
 def solution(mesh):

time: 67.4 us -> 67.2 us (level)
    transpose x3 -> x0, local copies, waits for them, and re-layouts: 5.57 us -> none  [the longest x2 4.1 us: joined(): array.reshape(groups, units, per, step, dim).transpose(1, 3, 0, 2, 4)]
    unnamed x6 -> x12, local copies, waits for them, and re-layouts: 2.93 us -> 8.16 us
where the time goes in v6:
time: 67.2 us; the launch traced here: 66.9 us
  Pallas kernels  58.1 us (86%)
  local copies, waits for them, and re-layouts  8.16 us (12%)
    pallas_call x1, Pallas kernels, body(): pl.pallas_call(functools.partial(kernel, size, reach), out_shape=(wide, w...  58.1 us
    unnamed x12, local copies, waits for them, and re-layouts  8.16 us

profile of v6, /device:TPU:0, one launch (start us, length us, event | category | flops | bytes accessed | tf_op | source)
XLA Modules:
  0.0 66.9 jit_solution(6849345087541866709)
XLA Ops:
  0.6 0.0 copy-start
  0.6 1.2 %copy-done = bf16[256,16,128]{2,1,0:T(8,128)(2,1)S(1)} copy-done((bf16[256,16,128]{2,1,0:T(8,128)(2,1)S(1)}, bf16[256,16,128]{2,1,0:T(8,128)(2,1)}, u32[]{:S(2)}) %copy-start) | copy-done | bytes 1048600
  1.9 0.0 copy-start.1
  1.9 1.0 %copy-done.1 = bf16[256,8,128]{2,1,0:T(8,128)(2,1)S(1)} copy-done((bf16[256,8,128]{2,1,0:T(8,128)(2,1)S(1)}, bf16[256,8,128]{2,1,0:T(8,128)(2,1)}, u32[]{:S(2)}) %copy-start.1) | copy-done | bytes 524312
  2.9 0.0 copy-start.2
  2.9 1.0 %copy-done.2 = bf16[256,8,128]{2,1,0:T(8,128)(2,1)S(1)} copy-done((bf16[256,8,128]{2,1,0:T(8,128)(2,1)S(1)}, bf16[256,8,128]{2,1,0:T(8,128)(2,1)}, u32[]{:S(2)}) %copy-start.2) | copy-done | bytes 524312
  3.9 0.0 copy-start.3
  3.9 0.7 copy-done.3
  4.6 58.1 %shard_map.84 = (bf16[256,16,128]{2,1,0:T(8,128)(2,1)S(1)}, bf16[256,16,128]{2,1,0:T(8,128)(2,1)S(1)}, bf16[8,256,128]{2,1,0:T(8,128)(2,1)S(1)}, bf16[8,256,128]{2,1,0:T(8,128)(2,1)S(1)}) custom-call(s32[16]{0:T(128)S(1)} %copy-done.3, bf16[256,16,128]{2,1,0:T(8,128)(2,1)S(1)} %copy-done, bf16[256,16,128]{2,1,0:T(8,128)(2,1)} %g_ref.1, ...), custom_call_target="tpu_custom_call" | custom-call | tf_op jit(solution)/shard_map/pallas_call | solution.py:224
  62.7 1.1 %copy.9 = bf16[256,8,128]{2,1,0:T(8,128)(2,1)} copy(bf16[256,8,128]{2,0,1:T(8,128)(2,1)S(1)} %bitcast.3) | data formatting | bytes 1048576
  63.9 1.1 %copy.10 = bf16[256,8,128]{2,1,0:T(8,128)(2,1)} copy(bf16[256,8,128]{2,0,1:T(8,128)(2,1)S(1)} %bitcast.2) | data formatting | bytes 1048576
  65.0 1.0 %copy.13 = bf16[256,16,128]{2,1,0:T(8,128)(2,1)} copy(bf16[256,16,128]{2,1,0:T(8,128)(2,1)S(1)} %get-tuple-element.20) | data formatting | bytes 2097152
  66.0 1.0 %copy.14 = bf16[256,16,128]{2,1,0:T(8,128)(2,1)} copy(bf16[256,16,128]{2,1,0:T(8,128)(2,1)S(1)} %get-tuple-element.21) | data formatting | bytes 2097152
Async XLA Ops:
  0.6 1.2 %copy-start = (bf16[256,16,128]{2,1,0:T(8,128)(2,1)S(1)}, bf16[256,16,128]{2,1,0:T(8,128)(2,1)}, u32[]{:S(2)}) copy-start(bf16[256,16,128]{2,1,0:T(8,128)(2,1)} %q_ref.1) | copy-start | bytes 3145732
  1.9 1.0 %copy-start.1 = (bf16[256,8,128]{2,1,0:T(8,128)(2,1)S(1)}, bf16[256,8,128]{2,1,0:T(8,128)(2,1)}, u32[]{:S(2)}) copy-start(bf16[256,8,128]{2,1,0:T(8,128)(2,1)} %k_ref.1) | copy-start | bytes 1572868
  2.9 1.0 %copy-start.2 = (bf16[256,8,128]{2,1,0:T(8,128)(2,1)S(1)}, bf16[256,8,128]{2,1,0:T(8,128)(2,1)}, u32[]{:S(2)}) copy-start(bf16[256,8,128]{2,1,0:T(8,128)(2,1)} %v_ref.1) | copy-start | bytes 1572868
  3.9 0.7 copy-start.3

commit v7 on v5

--- a/solution.py
+++ b/solution.py
@@ -72,7 +72,7 @@
         kv_all[g, 0, slot(0), :] = k_ref[g]
         kv_all[g, 1, slot(0), :] = v_ref[g]
 
-        for d in distances:
+        for d in reversed(distances):
             @pl.when(me + d < size)
             def _():
                 outward(d, g).start()
@@ -172,7 +172,7 @@
                 low = (reach - d) * rows + n * step
                 part[d - 1, g, 0, inner] = total(key_grad, low).astype(BF16)
                 part[d - 1, g, 1, inner] = total(value_grad, low).astype(BF16)
-        for d in distances:
+        for d in reversed(distances):
             @pl.when(me >= d)
             def _():
                 homeward(d, g).start()

time: 67.4 us -> 68.7 us (1.019)
  Pallas kernels: 58 us -> 59.3 us
    pallas_call x1, Pallas kernels: 58 us -> 59.3 us  [body(): pl.pallas_call(functools.partial(kernel, size, reach), out_shape=(wide, w...]
where the time goes in v7:
time: 68.7 us; the launch traced here: 68.5 us
  Pallas kernels  59.3 us (86%)
  local copies, waits for them, and re-layouts  8.5 us (12%)
    pallas_call x1, Pallas kernels, body(): pl.pallas_call(functools.partial(kernel, size, reach), out_shape=(wide, w...  59.3 us
    transpose x2, local copies, waits for them, and re-layouts, joined(): array.reshape(groups, units, per, step, dim).transpose(1, 3, 0, 2, 4)  4.1 us
    unnamed x6, local copies, waits for them, and re-layouts  2.93 us
    transpose x1, local copies, waits for them, and re-layouts, body(): values.transpose(1, 0, 2)  1.48 us

profile of v7, /device:TPU:0, one launch (start us, length us, event | category | flops | bytes accessed | tf_op | source)
XLA Modules:
  0.0 68.5 jit_solution(9402401400378364052)
XLA Ops:
  0.6 0.0 copy-start
  0.6 1.5 %copy_bitcast_fusion = (bf16[8,256,128]{2,1,0:T(8,128)(2,1)S(1)}, bf16[8,256,128]{2,1,0:T(8,128)(2,1)S(1)}) fusion(bf16[256,8,128]{2,1,0:T(8,128)(2,1)} %param.7, bf16[256,8,128]{2,1,0:T(8,128)(2,1)} %param.6), kind=kLoop, calls=%fused_computation | loop fusion | bytes 2097152 | tf_op jit(solution)/shard_map/transpose | solution.py:237
  2.1 0.0 copy-start.1
  2.1 0.0 copy-done
  2.2 0.6 copy-done.1
  2.8 59.3 %shard_map.84 = (bf16[8,2,256,128]{3,2,1,0:T(8,128)(2,1)S(1)}, bf16[8,2,256,128]{3,2,1,0:T(8,128)(2,1)S(1)}, bf16[8,256,128]{2,1,0:T(8,128)(2,1)S(1)}, bf16[8,256,128]{2,1,0:T(8,128)(2,1)S(1)}) custom-call(s32[16]{0:T(128)S(1)} %copy-done.1, bf16[256,16,128]{2,1,0:T(8,128)(2,1)S(1)} %copy-done, bf16[256,16,128]{2,1,0:T(8,128)(2,1)} %g_ref.1, ...), custom_call_target="tpu_custom_call" | custom-call | tf_op jit(solution)/shard_map/pallas_call | solution.py:219
  62.1 2.0 %copy.11 = bf16[2,128,8,2,128]{4,3,2,1,0:T(2,128)(2,1)} copy(bf16[2,128,8,2,128]{4,1,3,0,2:T(8,128)(2,1)S(1)} %bitcast.15) | data formatting | bytes 2097152 | tf_op jit(solution)/shard_map/transpose | solution.py:211
  64.1 2.0 %copy.12 = bf16[2,128,8,2,128]{4,3,2,1,0:T(2,128)(2,1)} copy(bf16[2,128,8,2,128]{4,1,3,0,2:T(8,128)(2,1)S(1)} %bitcast.14) | data formatting | bytes 2097152 | tf_op jit(solution)/shard_map/transpose | solution.py:211
  66.2 1.1 %copy.13 = bf16[256,8,128]{2,1,0:T(8,128)(2,1)} copy(bf16[256,8,128]{2,0,1:T(8,128)(2,1)S(1)} %bitcast.17) | data formatting | bytes 1048576
  67.3 1.1 %copy.14 = bf16[256,8,128]{2,1,0:T(8,128)(2,1)} copy(bf16[256,8,128]{2,0,1:T(8,128)(2,1)S(1)} %bitcast.16) | data formatting | bytes 1048576
Async XLA Ops:
  0.6 1.5 %copy-start = (bf16[256,16,128]{2,1,0:T(8,128)(2,1)S(1)}, bf16[256,16,128]{2,1,0:T(8,128)(2,1)}, u32[]{:S(2)}) copy-start(bf16[256,16,128]{2,1,0:T(8,128)(2,1)} %q_ref.1) | copy-start | bytes 3145732
  2.1 0.7 copy-start.1
